TPU v7x, 768 devices: a whole 4x8x12 slice. The times are simulated.
768 devices in a mesh: mp: 96 (over x, z, y_lo), station: 8 (over y_hi, core).
Axes of the slice: x: 4, y: 8 (y_hi: 4, y_lo: 2; y = y_hi * 2 + y_lo), z: 12, core: 2. Of those that a mesh axis runs over, the one named last changes fastest.
Arguments:
- p_now: float32 [768, 64, 128], P('mp'), may hold values from -2.7 to 2.7
- p_prev: float32 [768, 64, 128], P('mp'), may hold values from -2.7 to 2.7
- velocity: float32 [768, 64, 128], P('mp'), may hold values from 4 to 4.5
- density: float32 [768, 64, 128], P('mp'), may hold values from -6 to 6
- wavelet: float32 [16], replicated, may hold values from -4 to 4
- source_cell: int32 [1], replicated, may hold values from 0 to 6291455
- receiver_cells: int32 [256], replicated, may hold values from 0 to 49151
- station_cells: int32 [1024], P('station'), may hold values from 0 to 49151
- observed: float32 [1024], P('station'), may hold values from -6 to 6
Outputs:
- wavefield: float32 [768, 64, 128], P('mp')
- traces: float32 [16, 256], replicated
- gravity_residual: float32 [1024], P('station')
- density_gradient: float32 [768, 64, 128], P('mp', 'station')
- cross_gradient: float32 [3, 768, 64, 128], P(None, 'mp')
All inputs are finite; a program needn't handle non-finite values.
Results may differ from a plain program's by a relative error of at most 0.0036.
The roundings to bfloat16 on the way count: a program that leaves them out, or rounds other values in their place, can miss the bound.
Values sent between devices are 32-bit elements; how exact they have to be, the bound alone decides.
A program may use at most 32 MiB of HBM per device.

v0:
```python
import jax
import jax.numpy as jnp
from jax import lax
from jax.sharding import Mesh
from jax.sharding import PartitionSpec as P

MP = ("mp_0", "mp_1", "mp_2")


STENCIL = (-205.0 / 72.0, 8.0 / 5.0, -1.0 / 5.0, 8.0 / 315.0, -1.0 / 560.0)
TIME_RATIO = 0.1


def extended(cells, sides, width):
    for axis, dim in sides:
        count = lax.axis_size(axis)
        ends = count - 1
        head = lax.slice_in_dim(cells, 0, width, axis=dim)
        tail = lax.slice_in_dim(cells, cells.shape[dim] - width, cells.shape[dim], axis=dim)
        cells = jnp.concatenate(
            [
                lax.ppermute(tail, axis, [(i, (i + 1) % count) for i in range(ends)]),
                cells,
                lax.ppermute(head, axis, [((i + 1) % count, i) for i in range(ends)]),
            ],
            axis=dim,
        )
    return cells


def over_axes(x, axes):
    for axis in axes:
        x = lax.psum(x, axis)
    return x


def turned_gather(arrays, axis, dims):
    turned = [jnp.moveaxis(a, dim, 0) for a, dim in zip(arrays, dims)]
    widths = [t[0].size for t in turned]
    both = jnp.concatenate([t.reshape(-1, w) for t, w in zip(turned, widths)], axis=1)
    result = lax.all_gather(both, axis, axis=0, tiled=True)
    blocks = jnp.split(result, [sum(widths[:k]) for k in range(1, len(widths))], axis=1)
    return tuple(
        (
            jnp.moveaxis(b.reshape(-1, *t.shape[1:]), 0, dim)
            for b, t, dim in zip(blocks, turned, dims)
        )
    )


def stencil(padded, current):
    slab, lateral, vertical = current.shape
    result = 3.0 * STENCIL[0] * current
    for distance in range(1, 5):
        pairs = padded[4 + distance : 4 + distance + slab, 4 : 4 + lateral, 4 : 4 + vertical]
        pairs = (
            pairs + padded[4 - distance : 4 - distance + slab, 4 : 4 + lateral, 4 : 4 + vertical]
        )
        pairs = (
            pairs + padded[4 : 4 + slab, 4 + distance : 4 + distance + lateral, 4 : 4 + vertical]
        )
        pairs = (
            pairs + padded[4 : 4 + slab, 4 - distance : 4 - distance + lateral, 4 : 4 + vertical]
        )
        pairs = (
            pairs + padded[4 : 4 + slab, 4 : 4 + lateral, 4 + distance : 4 + distance + vertical]
        )
        pairs = (
            pairs + padded[4 : 4 + slab, 4 : 4 + lateral, 4 - distance : 4 - distance + vertical]
        )
        result = result + STENCIL[distance] * pairs
    return result


def kernel_tile(plane_x, station_x, station_y, cell_y, cell_z):
    delta_x = plane_x - station_x
    delta_y = cell_y[None, :] - station_y[:, None]
    radius_sq = (
        delta_x[:, None] * delta_x[:, None] + delta_y * delta_y + cell_z[None, :] * cell_z[None, :]
    )
    return (cell_z[None, :] / (radius_sq * jnp.sqrt(radius_sq))).astype(jnp.bfloat16)


def cross_terms(padded, slab, lateral, vertical):
    diff_x = (
        padded[:, 2 : 2 + slab, 1 : 1 + lateral, 1 : 1 + vertical]
        - padded[:, 0:slab, 1 : 1 + lateral, 1 : 1 + vertical]
    ) * 0.5
    diff_y = (
        padded[:, 1 : 1 + slab, 2 : 2 + lateral, 1 : 1 + vertical]
        - padded[:, 1 : 1 + slab, 0:lateral, 1 : 1 + vertical]
    ) * 0.5
    diff_z = (
        padded[:, 1 : 1 + slab, 1 : 1 + lateral, 2 : 2 + vertical]
        - padded[:, 1 : 1 + slab, 1 : 1 + lateral, 0:vertical]
    ) * 0.5
    first = diff_y[0] * diff_z[1] - diff_z[0] * diff_y[1]
    second = diff_z[0] * diff_x[1] - diff_x[0] * diff_z[1]
    third = diff_x[0] * diff_y[1] - diff_y[0] * diff_x[1]
    return jnp.stack([first, second, third])


def per_device(
    p_now, p_prev, velocity, density, wavelet, source_cell, receiver_cells, station_cells, observed
):
    slab, lateral, vertical = p_now.shape
    offset_x = lax.axis_index(MP) * slab
    courant = TIME_RATIO * velocity * (TIME_RATIO * velocity)
    offset_y = 0
    global_x = offset_x + jnp.arange(slab, dtype=jnp.int32)
    global_y = offset_y + jnp.arange(lateral, dtype=jnp.int32)
    flat_index = (
        global_x[:, None, None] * lateral + global_y[None, :, None]
    ) * vertical + jnp.arange(vertical, dtype=jnp.int32)[None, None, :]
    source_mask = (flat_index == source_cell[0]).astype(jnp.float32)
    receiver_x = receiver_cells // lateral
    receiver_y = receiver_cells % lateral
    inside = (
        (receiver_x >= offset_x)
        & (receiver_x < offset_x + slab)
        & (receiver_y >= offset_y)
        & (receiver_y < offset_y + lateral)
    )
    safe_index = jnp.where(inside, (receiver_x - offset_x) * lateral + (receiver_y - offset_y), 0)

    def advance(carry, pulse):
        present, earlier = carry
        padded = extended(present, ((MP, 0),), 4)
        padded = jnp.pad(padded, ((0, 0), (4, 4), (4, 4)))
        updated = 2.0 * present - earlier + courant * stencil(padded, present) + pulse * source_mask
        surface = updated[:, :, 0].reshape(-1)
        recorded = jnp.where(inside, surface[safe_index], 0.0)
        return ((updated, present), recorded)

    (last_field, unused), recorded_all = lax.scan(advance, (p_now, p_prev), wavelet)
    traces = over_axes(recorded_all, MP)
    stacked = jnp.stack([velocity, density])
    padded_model = extended(stacked, ((MP, 1),), 1)
    padded_model = jnp.pad(padded_model, ((0, 0), (0, 0), (1, 1), (1, 1)))
    cross_gradient = cross_terms(padded_model, slab, lateral, vertical)
    station_x = (station_cells // lateral).astype(jnp.float32)
    station_y = (station_cells % lateral).astype(jnp.float32)
    cell_y = (jnp.arange(lateral * vertical, dtype=jnp.int32) // vertical).astype(jnp.float32)
    cell_z = (jnp.arange(lateral * vertical, dtype=jnp.int32) % vertical).astype(jnp.float32) + 1.0
    planes = density.astype(jnp.bfloat16).reshape(slab, lateral * vertical)
    plane_xs = global_x.astype(jnp.float32)

    def forward(totals, packed):
        plane_x, plane = packed
        tile = kernel_tile(plane_x, station_x, station_y, cell_y, cell_z)
        return (totals + jnp.dot(tile, plane, preferred_element_type=jnp.float32), None)

    partial_value, unused_out = lax.scan(
        forward, jnp.zeros((station_cells.shape[0],), jnp.float32), (plane_xs, planes)
    )
    predicted = over_axes(partial_value, MP)
    gravity_residual = predicted - observed
    share_rows = lateral // lax.axis_size("station")
    every_residual, every_x, every_y = turned_gather(
        (gravity_residual, station_x, station_y), "station", (0, 0, 0)
    )
    every_low = every_residual.astype(jnp.bfloat16)
    share_index = jnp.arange(share_rows * vertical, dtype=jnp.int32)
    share_y = (lax.axis_index("station") * share_rows + share_index // vertical).astype(jnp.float32)
    share_z = (share_index % vertical).astype(jnp.float32) + 1.0

    def adjoint_rows(plane_x):
        tile = kernel_tile(plane_x, every_x, every_y, share_y, share_z)
        return jnp.dot(every_low, tile, preferred_element_type=jnp.float32)

    density_gradient = lax.map(adjoint_rows, plane_xs).reshape(slab, share_rows, vertical)
    return (last_field, traces, gravity_residual, density_gradient, cross_gradient)


def solution(mesh):
    split = Mesh(
        mesh.devices.reshape(4, 12, 2, mesh.shape["station"]), ("mp_0", "mp_1", "mp_2", "station")
    )
    return jax.shard_map(
        per_device,
        mesh=split,
        in_specs=(
            P(MP, None, None),
            P(MP, None, None),
            P(MP, None, None),
            P(MP, None, None),
            P(),
            P(),
            P(),
            P("station"),
            P("station"),
        ),
        out_specs=(
            P(MP, None, None),
            P(),
            P("station"),
            P(MP, "station", None),
            P(None, MP, None, None),
        ),
        check_vma=False,
    )
```

profile of v0, /device:TPU:1, one launch (start us, length us, event | category | flops | bytes accessed | tf_op | source)
XLA Modules:
  0.0 440.2 jit_solution(17678993954866940312)
XLA Ops:
  2.8 4.7 %collective-permute-start.2 = (f32[2,1,64,128]{3,2,1,0:T(8,128)S(1)}, f32[2,1,64,128]{3,2,1,0:T(8,128)S(1)}, u32[]{:S(2)}, u32[]{:S(2)}) collective-permute-start(f32[2,1,64,128]{3,2,1,0:T(8,128)S(1)} %get-tuple-element.432), channel_id=1, source_target_pairs={{0,8},{8,16},{16,24},{24,32},{32,40},{40,48},{48,56},{56,64},{64,7... | collective-permute-start | bytes 196616 | tf_op jit(solution)/shard_map/ppermute | solution.py:22
  7.9 28.2 %while.43 = (s32[]{:T(128)}, f32[128]{0:T(128)S(1)}, f32[8]{0:T(128)S(1)}, f32[128]{0:T(128)S(1)}, f32[128]{0:T(128)S(1)}, /*index=5*/bf16[8,8192]{1,0:T(8,128)(2,1)S(1)}, s32[]{:T(128)}, s32[]{:T(128)}) while((s32[]{:T(128)}, f32[128]{0:T(128)S(1)}, f32[8]{0:T(128)S(1)}, f32[128]{0:T(128)S(1)}, f32[128]{0:T(128)S(1)}, ...), condition=%wide.region_6.7_spmd.clone, body=%wide.region_5.6_spmd.clone.sunk | while | flops 9650691 | bytes 232571 | solution.py:153
  36.2 255.7 %while.41 = (s32[]{:T(128)}, f32[8,64,128]{2,1,0:T(8,128)S(1)}, f32[8,64,128]{2,1,0:T(8,128)S(1)}, f32[16,256]{1,0:T(8,128)S(1)}, f32[8,64,128]{2,1,0:T(8,128)S(...) while((s32[]{:T(128)}, f32[8,64,128]{2,1,0:T(8,128)S(1)}, ...), condition=%wide.region_1.2_spmd.clone, body=%wide.region_0.1_spmd.clone.sunk | while | flops 4776962 | bytes 12448229 | solution.py:135
  37.5 4.9 %collective-permute-start.1 = (f32[4,64,128]{2,1,0:T(8,128)S(1)}, f32[4,64,128]{2,1,0:T(8,128)S(1)}, u32[]{:S(2)}, u32[]{:S(2)}) collective-permute-start(f32[4,64,128]{2,1,0:T(8,128)S(1)} %get-tuple-element.575), channel_id=1, source_target_pairs={{0,8},{8,16},{16,24},{24,32},{32,40},{40,48},{48,56},{56,64},{64,7... | collective-permute-start | bytes 393224 | tf_op jit(solution)/shard_map/while/body/eval_jaxpr/ppermute | solution.py:22
  51.2 4.6 %collective-permute-start.1 = (f32[4,64,128]{2,1,0:T(8,128)S(1)}, f32[4,64,128]{2,1,0:T(8,128)S(1)}, u32[]{:S(2)}, u32[]{:S(2)}) collective-permute-start(f32[4,64,128]{2,1,0:T(8,128)S(1)} %get-tuple-element.575), channel_id=1, source_target_pairs={{0,8},{8,16},{16,24},{24,32},{32,40},{40,48},{48,56},{56,64},{64,7... | collective-permute-start | bytes 393224 | tf_op jit(solution)/shard_map/while/body/eval_jaxpr/ppermute | solution.py:22
  65.0 4.6 %collective-permute-start.1 = (f32[4,64,128]{2,1,0:T(8,128)S(1)}, f32[4,64,128]{2,1,0:T(8,128)S(1)}, u32[]{:S(2)}, u32[]{:S(2)}) collective-permute-start(f32[4,64,128]{2,1,0:T(8,128)S(1)} %get-tuple-element.575), channel_id=1, source_target_pairs={{0,8},{8,16},{16,24},{24,32},{32,40},{40,48},{48,56},{56,64},{64,7... | collective-permute-start | bytes 393224 | tf_op jit(solution)/shard_map/while/body/eval_jaxpr/ppermute | solution.py:22
  78.8 4.6 %collective-permute-start.1 = (f32[4,64,128]{2,1,0:T(8,128)S(1)}, f32[4,64,128]{2,1,0:T(8,128)S(1)}, u32[]{:S(2)}, u32[]{:S(2)}) collective-permute-start(f32[4,64,128]{2,1,0:T(8,128)S(1)} %get-tuple-element.575), channel_id=1, source_target_pairs={{0,8},{8,16},{16,24},{24,32},{32,40},{40,48},{48,56},{56,64},{64,7... | collective-permute-start | bytes 393224 | tf_op jit(solution)/shard_map/while/body/eval_jaxpr/ppermute | solution.py:22
  93.4 4.4 %collective-permute-start.1 = (f32[4,64,128]{2,1,0:T(8,128)S(1)}, f32[4,64,128]{2,1,0:T(8,128)S(1)}, u32[]{:S(2)}, u32[]{:S(2)}) collective-permute-start(f32[4,64,128]{2,1,0:T(8,128)S(1)} %get-tuple-element.575), channel_id=1, source_target_pairs={{0,8},{8,16},{16,24},{24,32},{32,40},{40,48},{48,56},{56,64},{64,7... | collective-permute-start | bytes 393224 | tf_op jit(solution)/shard_map/while/body/eval_jaxpr/ppermute | solution.py:22
  98.4 4.8 %collective-permute-done.1 = f32[4,64,128]{2,1,0:T(8,128)S(1)} collective-permute-done((f32[4,64,128]{2,1,0:T(8,128)S(1)}, f32[4,64,128]{2,1,0:T(8,128)S(1)}, u32[]{:S(2)}, u32[]{:S(2)}) %collective-permute-start.1) | collective-permute-done | bytes 131104 | tf_op jit(solution)/shard_map/while/body/eval_jaxpr/ppermute | solution.py:22
  109.8 4.7 %collective-permute-start.1 = (f32[4,64,128]{2,1,0:T(8,128)S(1)}, f32[4,64,128]{2,1,0:T(8,128)S(1)}, u32[]{:S(2)}, u32[]{:S(2)}) collective-permute-start(f32[4,64,128]{2,1,0:T(8,128)S(1)} %get-tuple-element.575), channel_id=1, source_target_pairs={{0,8},{8,16},{16,24},{24,32},{32,40},{40,48},{48,56},{56,64},{64,7... | collective-permute-start | bytes 393224 | tf_op jit(solution)/shard_map/while/body/eval_jaxpr/ppermute | solution.py:22
  126.1 4.7 %collective-permute-start.1 = (f32[4,64,128]{2,1,0:T(8,128)S(1)}, f32[4,64,128]{2,1,0:T(8,128)S(1)}, u32[]{:S(2)}, u32[]{:S(2)}) collective-permute-start(f32[4,64,128]{2,1,0:T(8,128)S(1)} %get-tuple-element.575), channel_id=1, source_target_pairs={{0,8},{8,16},{16,24},{24,32},{32,40},{40,48},{48,56},{56,64},{64,7... | collective-permute-start | bytes 393224 | tf_op jit(solution)/shard_map/while/body/eval_jaxpr/ppermute | solution.py:22
  142.3 4.7 %collective-permute-start.1 = (f32[4,64,128]{2,1,0:T(8,128)S(1)}, f32[4,64,128]{2,1,0:T(8,128)S(1)}, u32[]{:S(2)}, u32[]{:S(2)}) collective-permute-start(f32[4,64,128]{2,1,0:T(8,128)S(1)} %get-tuple-element.575), channel_id=1, source_target_pairs={{0,8},{8,16},{16,24},{24,32},{32,40},{40,48},{48,56},{56,64},{64,7... | collective-permute-start | bytes 393224 | tf_op jit(solution)/shard_map/while/body/eval_jaxpr/ppermute | solution.py:22
  158.6 4.7 %collective-permute-start.1 = (f32[4,64,128]{2,1,0:T(8,128)S(1)}, f32[4,64,128]{2,1,0:T(8,128)S(1)}, u32[]{:S(2)}, u32[]{:S(2)}) collective-permute-start(f32[4,64,128]{2,1,0:T(8,128)S(1)} %get-tuple-element.575), channel_id=1, source_target_pairs={{0,8},{8,16},{16,24},{24,32},{32,40},{40,48},{48,56},{56,64},{64,7... | collective-permute-start | bytes 393224 | tf_op jit(solution)/shard_map/while/body/eval_jaxpr/ppermute | solution.py:22
  174.9 4.7 %collective-permute-start.1 = (f32[4,64,128]{2,1,0:T(8,128)S(1)}, f32[4,64,128]{2,1,0:T(8,128)S(1)}, u32[]{:S(2)}, u32[]{:S(2)}) collective-permute-start(f32[4,64,128]{2,1,0:T(8,128)S(1)} %get-tuple-element.575), channel_id=1, source_target_pairs={{0,8},{8,16},{16,24},{24,32},{32,40},{40,48},{48,56},{56,64},{64,7... | collective-permute-start | bytes 393224 | tf_op jit(solution)/shard_map/while/body/eval_jaxpr/ppermute | solution.py:22
  180.2 4.6 %collective-permute-done.1 = f32[4,64,128]{2,1,0:T(8,128)S(1)} collective-permute-done((f32[4,64,128]{2,1,0:T(8,128)S(1)}, f32[4,64,128]{2,1,0:T(8,128)S(1)}, u32[]{:S(2)}, u32[]{:S(2)}) %collective-permute-start.1) | collective-permute-done | bytes 131104 | tf_op jit(solution)/shard_map/while/body/eval_jaxpr/ppermute | solution.py:22
  191.4 4.7 %collective-permute-start.1 = (f32[4,64,128]{2,1,0:T(8,128)S(1)}, f32[4,64,128]{2,1,0:T(8,128)S(1)}, u32[]{:S(2)}, u32[]{:S(2)}) collective-permute-start(f32[4,64,128]{2,1,0:T(8,128)S(1)} %get-tuple-element.575), channel_id=1, source_target_pairs={{0,8},{8,16},{16,24},{24,32},{32,40},{40,48},{48,56},{56,64},{64,7... | collective-permute-start | bytes 393224 | tf_op jit(solution)/shard_map/while/body/eval_jaxpr/ppermute | solution.py:22
  196.8 4.6 %collective-permute-done.1 = f32[4,64,128]{2,1,0:T(8,128)S(1)} collective-permute-done((f32[4,64,128]{2,1,0:T(8,128)S(1)}, f32[4,64,128]{2,1,0:T(8,128)S(1)}, u32[]{:S(2)}, u32[]{:S(2)}) %collective-permute-start.1) | collective-permute-done | bytes 131104 | tf_op jit(solution)/shard_map/while/body/eval_jaxpr/ppermute | solution.py:22
  207.9 4.7 %collective-permute-start.1 = (f32[4,64,128]{2,1,0:T(8,128)S(1)}, f32[4,64,128]{2,1,0:T(8,128)S(1)}, u32[]{:S(2)}, u32[]{:S(2)}) collective-permute-start(f32[4,64,128]{2,1,0:T(8,128)S(1)} %get-tuple-element.575), channel_id=1, source_target_pairs={{0,8},{8,16},{16,24},{24,32},{32,40},{40,48},{48,56},{56,64},{64,7... | collective-permute-start | bytes 393224 | tf_op jit(solution)/shard_map/while/body/eval_jaxpr/ppermute | solution.py:22
  213.3 4.8 %collective-permute-done.1 = f32[4,64,128]{2,1,0:T(8,128)S(1)} collective-permute-done((f32[4,64,128]{2,1,0:T(8,128)S(1)}, f32[4,64,128]{2,1,0:T(8,128)S(1)}, u32[]{:S(2)}, u32[]{:S(2)}) %collective-permute-start.1) | collective-permute-done | bytes 131104 | tf_op jit(solution)/shard_map/while/body/eval_jaxpr/ppermute | solution.py:22
  224.7 4.7 %collective-permute-start.1 = (f32[4,64,128]{2,1,0:T(8,128)S(1)}, f32[4,64,128]{2,1,0:T(8,128)S(1)}, u32[]{:S(2)}, u32[]{:S(2)}) collective-permute-start(f32[4,64,128]{2,1,0:T(8,128)S(1)} %get-tuple-element.575), channel_id=1, source_target_pairs={{0,8},{8,16},{16,24},{24,32},{32,40},{40,48},{48,56},{56,64},{64,7... | collective-permute-start | bytes 393224 | tf_op jit(solution)/shard_map/while/body/eval_jaxpr/ppermute | solution.py:22
  230.0 5.2 %collective-permute-done.1 = f32[4,64,128]{2,1,0:T(8,128)S(1)} collective-permute-done((f32[4,64,128]{2,1,0:T(8,128)S(1)}, f32[4,64,128]{2,1,0:T(8,128)S(1)}, u32[]{:S(2)}, u32[]{:S(2)}) %collective-permute-start.1) | collective-permute-done | bytes 131104 | tf_op jit(solution)/shard_map/while/body/eval_jaxpr/ppermute | solution.py:22
  241.8 4.7 %collective-permute-start.1 = (f32[4,64,128]{2,1,0:T(8,128)S(1)}, f32[4,64,128]{2,1,0:T(8,128)S(1)}, u32[]{:S(2)}, u32[]{:S(2)}) collective-permute-start(f32[4,64,128]{2,1,0:T(8,128)S(1)} %get-tuple-element.575), channel_id=1, source_target_pairs={{0,8},{8,16},{16,24},{24,32},{32,40},{40,48},{48,56},{56,64},{64,7... | collective-permute-start | bytes 393224 | tf_op jit(solution)/shard_map/while/body/eval_jaxpr/ppermute | solution.py:22
  247.2 5.2 %collective-permute-done.1 = f32[4,64,128]{2,1,0:T(8,128)S(1)} collective-permute-done((f32[4,64,128]{2,1,0:T(8,128)S(1)}, f32[4,64,128]{2,1,0:T(8,128)S(1)}, u32[]{:S(2)}, u32[]{:S(2)}) %collective-permute-start.1) | collective-permute-done | bytes 131104 | tf_op jit(solution)/shard_map/while/body/eval_jaxpr/ppermute | solution.py:22
  258.9 4.7 %collective-permute-start.1 = (f32[4,64,128]{2,1,0:T(8,128)S(1)}, f32[4,64,128]{2,1,0:T(8,128)S(1)}, u32[]{:S(2)}, u32[]{:S(2)}) collective-permute-start(f32[4,64,128]{2,1,0:T(8,128)S(1)} %get-tuple-element.575), channel_id=1, source_target_pairs={{0,8},{8,16},{16,24},{24,32},{32,40},{40,48},{48,56},{56,64},{64,7... | collective-permute-start | bytes 393224 | tf_op jit(solution)/shard_map/while/body/eval_jaxpr/ppermute | solution.py:22
  264.3 5.2 %collective-permute-done.1 = f32[4,64,128]{2,1,0:T(8,128)S(1)} collective-permute-done((f32[4,64,128]{2,1,0:T(8,128)S(1)}, f32[4,64,128]{2,1,0:T(8,128)S(1)}, u32[]{:S(2)}, u32[]{:S(2)}) %collective-permute-start.1) | collective-permute-done | bytes 131104 | tf_op jit(solution)/shard_map/while/body/eval_jaxpr/ppermute | solution.py:22
  276.1 4.7 %collective-permute-start.1 = (f32[4,64,128]{2,1,0:T(8,128)S(1)}, f32[4,64,128]{2,1,0:T(8,128)S(1)}, u32[]{:S(2)}, u32[]{:S(2)}) collective-permute-start(f32[4,64,128]{2,1,0:T(8,128)S(1)} %get-tuple-element.575), channel_id=1, source_target_pairs={{0,8},{8,16},{16,24},{24,32},{32,40},{40,48},{48,56},{56,64},{64,7... | collective-permute-start | bytes 393224 | tf_op jit(solution)/shard_map/while/body/eval_jaxpr/ppermute | solution.py:22
  281.4 5.2 %collective-permute-done.1 = f32[4,64,128]{2,1,0:T(8,128)S(1)} collective-permute-done((f32[4,64,128]{2,1,0:T(8,128)S(1)}, f32[4,64,128]{2,1,0:T(8,128)S(1)}, u32[]{:S(2)}, u32[]{:S(2)}) %collective-permute-start.1) | collective-permute-done | bytes 131104 | tf_op jit(solution)/shard_map/while/body/eval_jaxpr/ppermute | solution.py:22
  291.9 32.7 %all-reduce.3 = (f32[16,256]{1,0:T(8,128)S(1)}, f32[128]{0:T(128)S(1)}) all-reduce(f32[16,256]{1,0:T(8,128)S(1)} %get-tuple-element.278, f32[128]{0:T(128)S(1)} %get-tuple-element.279), channel_id=1, replica_groups=mesh['mp_0'=4,'mp_1'=12,'mp_2'=2,'station'=8] {'mp_0'}, use_global_device_ids=true, to_apply=%region_2.3 | all-reduce | flops 4224 | bytes 33792 | tf_op jit(solution)/shard_map/psum | solution.py:33
  324.6 39.0 %all-reduce.2 = (f32[16,256]{1,0:T(8,128)S(1)}, f32[128]{0:T(128)S(1)}) all-reduce(f32[16,256]{1,0:T(8,128)S(1)} %get-tuple-element.414, f32[128]{0:T(128)S(1)} %get-tuple-element.415), channel_id=1, replica_groups=mesh['mp_0'=4,'mp_1'=12,'mp_2'=2,'station'=8] {'mp_1'}, use_global_device_ids=true, to_apply=%region_3.4 | all-reduce | flops 4224 | bytes 33792 | tf_op jit(solution)/shard_map/psum | solution.py:33
  363.5 8.3 %all-reduce.4 = (f32[16,256]{1,0:T(8,128)}, f32[128]{0:T(128)S(1)}) all-reduce(f32[16,256]{1,0:T(8,128)S(1)} %get-tuple-element.412, f32[128]{0:T(128)S(1)} %get-tuple-element.413), channel_id=1, replica_groups=mesh['mp_0'=4,'mp_1'=12,'mp_2'=2,'station'=8] {'mp_2'}, use_global_device_ids=true, to_apply=%region_4.5 | all-reduce | flops 4224 | bytes 33792 | tf_op jit(solution)/shard_map/psum | solution.py:33
  371.9 36.9 %all_gather.3 = f32[1024,3]{0,1:T(4,128)S(1)} all-gather(f32[128,3]{0,1:T(4,128)S(1)} %pad_maximum_fusion.7), channel_id=1, replica_groups=mesh['mp_0'=4,'mp_1'=12,'mp_2'=2,'station'=8] {'station'}, dimensions={0}, use_global_device_ids=true | all-gather | bytes 13824 | tf_op jit(solution)/shard_map/all_gather | solution.py:41
  408.9 28.6 %while.42 = (s32[]{:T(128)}, f32[8,1024]{1,0:T(8,128)S(1)}, f32[8]{0:T(128)S(1)}, f32[1024]{0:T(1024)S(1)}, f32[1024,1]{0,1:T(1,128)S(1)}, /*index=5*/bf16[1024]...) while((s32[]{:T(128)}, f32[8,1024]{1,0:T(8,128)S(1)}, f32[8]{0:T(128)S(1)}, ...), condition=%wide.region_11.12_spmd.clone, body=%wide.region_10.11_spmd.clone.sunk | while | flops 9466882 | bytes 59517 | solution.py:171
  (443 shorter events, 200.2 us)
Async XLA Ops:
  1.5 436.6 %collective-permute-start.3 = (f32[2,1,64,128]{3,2,1,0:T(8,128)S(1)}, f32[2,1,64,128]{3,2,1,0:T(8,128)S(1)}, u32[]{:S(2)}, u32[]{:S(2)}) collective-permute-start(f32[2,1,64,128]{3,2,1,0:T(8,128)S(1)} %get-tuple-element.431), channel_id=1, source_target_pairs={{8,0},{16,8},{24,16},{32,24},{40,32},{48,40},{56,48},{64,56},{72,6... | collective-permute-start | bytes 196616 | tf_op jit(solution)/shard_map/ppermute | solution.py:24
  2.8 435.3 %collective-permute-start.2 = (f32[2,1,64,128]{3,2,1,0:T(8,128)S(1)}, f32[2,1,64,128]{3,2,1,0:T(8,128)S(1)}, u32[]{:S(2)}, u32[]{:S(2)}) collective-permute-start(f32[2,1,64,128]{3,2,1,0:T(8,128)S(1)} %get-tuple-element.432), channel_id=1, source_target_pairs={{0,8},{8,16},{16,24},{24,32},{32,40},{40,48},{48,56},{56,64},{64,7... | collective-permute-start | bytes 196616 | tf_op jit(solution)/shard_map/ppermute | solution.py:22
  36.2 8.5 %collective-permute-start = (f32[4,64,128]{2,1,0:T(8,128)S(1)}, f32[4,64,128]{2,1,0:T(8,128)S(1)}, u32[]{:S(2)}, u32[]{:S(2)}) collective-permute-start(f32[4,64,128]{2,1,0:T(8,128)S(1)} %get-tuple-element.574), channel_id=1, source_target_pairs={{8,0},{16,8},{24,16},{32,24},{40,32},{48,40},{56,48},{64,56},{72,6... | collective-permute-start | bytes 393224 | tf_op jit(solution)/shard_map/while/body/eval_jaxpr/ppermute | solution.py:24
  49.9 8.6 %collective-permute-start = (f32[4,64,128]{2,1,0:T(8,128)S(1)}, f32[4,64,128]{2,1,0:T(8,128)S(1)}, u32[]{:S(2)}, u32[]{:S(2)}) collective-permute-start(f32[4,64,128]{2,1,0:T(8,128)S(1)} %get-tuple-element.574), channel_id=1, source_target_pairs={{8,0},{16,8},{24,16},{32,24},{40,32},{48,40},{56,48},{64,56},{72,6... | collective-permute-start | bytes 393224 | tf_op jit(solution)/shard_map/while/body/eval_jaxpr/ppermute | solution.py:24
  51.2 7.2 %collective-permute-start.1 = (f32[4,64,128]{2,1,0:T(8,128)S(1)}, f32[4,64,128]{2,1,0:T(8,128)S(1)}, u32[]{:S(2)}, u32[]{:S(2)}) collective-permute-start(f32[4,64,128]{2,1,0:T(8,128)S(1)} %get-tuple-element.575), channel_id=1, source_target_pairs={{0,8},{8,16},{16,24},{24,32},{32,40},{40,48},{48,56},{56,64},{64,7... | collective-permute-start | bytes 393224 | tf_op jit(solution)/shard_map/while/body/eval_jaxpr/ppermute | solution.py:22
  63.7 8.6 %collective-permute-start = (f32[4,64,128]{2,1,0:T(8,128)S(1)}, f32[4,64,128]{2,1,0:T(8,128)S(1)}, u32[]{:S(2)}, u32[]{:S(2)}) collective-permute-start(f32[4,64,128]{2,1,0:T(8,128)S(1)} %get-tuple-element.574), channel_id=1, source_target_pairs={{8,0},{16,8},{24,16},{32,24},{40,32},{48,40},{56,48},{64,56},{72,6... | collective-permute-start | bytes 393224 | tf_op jit(solution)/shard_map/while/body/eval_jaxpr/ppermute | solution.py:24
  77.5 9.4 %collective-permute-start = (f32[4,64,128]{2,1,0:T(8,128)S(1)}, f32[4,64,128]{2,1,0:T(8,128)S(1)}, u32[]{:S(2)}, u32[]{:S(2)}) collective-permute-start(f32[4,64,128]{2,1,0:T(8,128)S(1)} %get-tuple-element.574), channel_id=1, source_target_pairs={{8,0},{16,8},{24,16},{32,24},{40,32},{48,40},{56,48},{64,56},{72,6... | collective-permute-start | bytes 393224 | tf_op jit(solution)/shard_map/while/body/eval_jaxpr/ppermute | solution.py:24
  78.8 8.0 %collective-permute-start.1 = (f32[4,64,128]{2,1,0:T(8,128)S(1)}, f32[4,64,128]{2,1,0:T(8,128)S(1)}, u32[]{:S(2)}, u32[]{:S(2)}) collective-permute-start(f32[4,64,128]{2,1,0:T(8,128)S(1)} %get-tuple-element.575), channel_id=1, source_target_pairs={{0,8},{8,16},{16,24},{24,32},{32,40},{40,48},{48,56},{56,64},{64,7... | collective-permute-start | bytes 393224 | tf_op jit(solution)/shard_map/while/body/eval_jaxpr/ppermute | solution.py:22
  92.1 11.2 %collective-permute-start = (f32[4,64,128]{2,1,0:T(8,128)S(1)}, f32[4,64,128]{2,1,0:T(8,128)S(1)}, u32[]{:S(2)}, u32[]{:S(2)}) collective-permute-start(f32[4,64,128]{2,1,0:T(8,128)S(1)} %get-tuple-element.574), channel_id=1, source_target_pairs={{8,0},{16,8},{24,16},{32,24},{40,32},{48,40},{56,48},{64,56},{72,6... | collective-permute-start | bytes 393224 | tf_op jit(solution)/shard_map/while/body/eval_jaxpr/ppermute | solution.py:24
  93.4 9.8 %collective-permute-start.1 = (f32[4,64,128]{2,1,0:T(8,128)S(1)}, f32[4,64,128]{2,1,0:T(8,128)S(1)}, u32[]{:S(2)}, u32[]{:S(2)}) collective-permute-start(f32[4,64,128]{2,1,0:T(8,128)S(1)} %get-tuple-element.575), channel_id=1, source_target_pairs={{0,8},{8,16},{16,24},{24,32},{32,40},{40,48},{48,56},{56,64},{64,7... | collective-permute-start | bytes 393224 | tf_op jit(solution)/shard_map/while/body/eval_jaxpr/ppermute | solution.py:22
  108.5 11.1 %collective-permute-start = (f32[4,64,128]{2,1,0:T(8,128)S(1)}, f32[4,64,128]{2,1,0:T(8,128)S(1)}, u32[]{:S(2)}, u32[]{:S(2)}) collective-permute-start(f32[4,64,128]{2,1,0:T(8,128)S(1)} %get-tuple-element.574), channel_id=1, source_target_pairs={{8,0},{16,8},{24,16},{32,24},{40,32},{48,40},{56,48},{64,56},{72,6... | collective-permute-start | bytes 393224 | tf_op jit(solution)/shard_map/while/body/eval_jaxpr/ppermute | solution.py:24
  109.8 9.7 %collective-permute-start.1 = (f32[4,64,128]{2,1,0:T(8,128)S(1)}, f32[4,64,128]{2,1,0:T(8,128)S(1)}, u32[]{:S(2)}, u32[]{:S(2)}) collective-permute-start(f32[4,64,128]{2,1,0:T(8,128)S(1)} %get-tuple-element.575), channel_id=1, source_target_pairs={{0,8},{8,16},{16,24},{24,32},{32,40},{40,48},{48,56},{56,64},{64,7... | collective-permute-start | bytes 393224 | tf_op jit(solution)/shard_map/while/body/eval_jaxpr/ppermute | solution.py:22
  124.8 11.1 %collective-permute-start = (f32[4,64,128]{2,1,0:T(8,128)S(1)}, f32[4,64,128]{2,1,0:T(8,128)S(1)}, u32[]{:S(2)}, u32[]{:S(2)}) collective-permute-start(f32[4,64,128]{2,1,0:T(8,128)S(1)} %get-tuple-element.574), channel_id=1, source_target_pairs={{8,0},{16,8},{24,16},{32,24},{40,32},{48,40},{56,48},{64,56},{72,6... | collective-permute-start | bytes 393224 | tf_op jit(solution)/shard_map/while/body/eval_jaxpr/ppermute | solution.py:24
  126.1 9.7 %collective-permute-start.1 = (f32[4,64,128]{2,1,0:T(8,128)S(1)}, f32[4,64,128]{2,1,0:T(8,128)S(1)}, u32[]{:S(2)}, u32[]{:S(2)}) collective-permute-start(f32[4,64,128]{2,1,0:T(8,128)S(1)} %get-tuple-element.575), channel_id=1, source_target_pairs={{0,8},{8,16},{16,24},{24,32},{32,40},{40,48},{48,56},{56,64},{64,7... | collective-permute-start | bytes 393224 | tf_op jit(solution)/shard_map/while/body/eval_jaxpr/ppermute | solution.py:22
  141.0 11.1 %collective-permute-start = (f32[4,64,128]{2,1,0:T(8,128)S(1)}, f32[4,64,128]{2,1,0:T(8,128)S(1)}, u32[]{:S(2)}, u32[]{:S(2)}) collective-permute-start(f32[4,64,128]{2,1,0:T(8,128)S(1)} %get-tuple-element.574), channel_id=1, source_target_pairs={{8,0},{16,8},{24,16},{32,24},{40,32},{48,40},{56,48},{64,56},{72,6... | collective-permute-start | bytes 393224 | tf_op jit(solution)/shard_map/while/body/eval_jaxpr/ppermute | solution.py:24
  142.3 9.7 %collective-permute-start.1 = (f32[4,64,128]{2,1,0:T(8,128)S(1)}, f32[4,64,128]{2,1,0:T(8,128)S(1)}, u32[]{:S(2)}, u32[]{:S(2)}) collective-permute-start(f32[4,64,128]{2,1,0:T(8,128)S(1)} %get-tuple-element.575), channel_id=1, source_target_pairs={{0,8},{8,16},{16,24},{24,32},{32,40},{40,48},{48,56},{56,64},{64,7... | collective-permute-start | bytes 393224 | tf_op jit(solution)/shard_map/while/body/eval_jaxpr/ppermute | solution.py:22
  157.3 11.1 %collective-permute-start = (f32[4,64,128]{2,1,0:T(8,128)S(1)}, f32[4,64,128]{2,1,0:T(8,128)S(1)}, u32[]{:S(2)}, u32[]{:S(2)}) collective-permute-start(f32[4,64,128]{2,1,0:T(8,128)S(1)} %get-tuple-element.574), channel_id=1, source_target_pairs={{8,0},{16,8},{24,16},{32,24},{40,32},{48,40},{56,48},{64,56},{72,6... | collective-permute-start | bytes 393224 | tf_op jit(solution)/shard_map/while/body/eval_jaxpr/ppermute | solution.py:24
  158.6 9.7 %collective-permute-start.1 = (f32[4,64,128]{2,1,0:T(8,128)S(1)}, f32[4,64,128]{2,1,0:T(8,128)S(1)}, u32[]{:S(2)}, u32[]{:S(2)}) collective-permute-start(f32[4,64,128]{2,1,0:T(8,128)S(1)} %get-tuple-element.575), channel_id=1, source_target_pairs={{0,8},{8,16},{16,24},{24,32},{32,40},{40,48},{48,56},{56,64},{64,7... | collective-permute-start | bytes 393224 | tf_op jit(solution)/shard_map/while/body/eval_jaxpr/ppermute | solution.py:22
  173.6 11.3 %collective-permute-start = (f32[4,64,128]{2,1,0:T(8,128)S(1)}, f32[4,64,128]{2,1,0:T(8,128)S(1)}, u32[]{:S(2)}, u32[]{:S(2)}) collective-permute-start(f32[4,64,128]{2,1,0:T(8,128)S(1)} %get-tuple-element.574), channel_id=1, source_target_pairs={{8,0},{16,8},{24,16},{32,24},{40,32},{48,40},{56,48},{64,56},{72,6... | collective-permute-start | bytes 393224 | tf_op jit(solution)/shard_map/while/body/eval_jaxpr/ppermute | solution.py:24
  174.9 10.0 %collective-permute-start.1 = (f32[4,64,128]{2,1,0:T(8,128)S(1)}, f32[4,64,128]{2,1,0:T(8,128)S(1)}, u32[]{:S(2)}, u32[]{:S(2)}) collective-permute-start(f32[4,64,128]{2,1,0:T(8,128)S(1)} %get-tuple-element.575), channel_id=1, source_target_pairs={{0,8},{8,16},{16,24},{24,32},{32,40},{40,48},{48,56},{56,64},{64,7... | collective-permute-start | bytes 393224 | tf_op jit(solution)/shard_map/while/body/eval_jaxpr/ppermute | solution.py:22
  190.1 11.3 %collective-permute-start = (f32[4,64,128]{2,1,0:T(8,128)S(1)}, f32[4,64,128]{2,1,0:T(8,128)S(1)}, u32[]{:S(2)}, u32[]{:S(2)}) collective-permute-start(f32[4,64,128]{2,1,0:T(8,128)S(1)} %get-tuple-element.574), channel_id=1, source_target_pairs={{8,0},{16,8},{24,16},{32,24},{40,32},{48,40},{56,48},{64,56},{72,6... | collective-permute-start | bytes 393224 | tf_op jit(solution)/shard_map/while/body/eval_jaxpr/ppermute | solution.py:24
  191.4 10.0 %collective-permute-start.1 = (f32[4,64,128]{2,1,0:T(8,128)S(1)}, f32[4,64,128]{2,1,0:T(8,128)S(1)}, u32[]{:S(2)}, u32[]{:S(2)}) collective-permute-start(f32[4,64,128]{2,1,0:T(8,128)S(1)} %get-tuple-element.575), channel_id=1, source_target_pairs={{0,8},{8,16},{16,24},{24,32},{32,40},{40,48},{48,56},{56,64},{64,7... | collective-permute-start | bytes 393224 | tf_op jit(solution)/shard_map/while/body/eval_jaxpr/ppermute | solution.py:22
  206.6 11.6 %collective-permute-start = (f32[4,64,128]{2,1,0:T(8,128)S(1)}, f32[4,64,128]{2,1,0:T(8,128)S(1)}, u32[]{:S(2)}, u32[]{:S(2)}) collective-permute-start(f32[4,64,128]{2,1,0:T(8,128)S(1)} %get-tuple-element.574), channel_id=1, source_target_pairs={{8,0},{16,8},{24,16},{32,24},{40,32},{48,40},{56,48},{64,56},{72,6... | collective-permute-start | bytes 393224 | tf_op jit(solution)/shard_map/while/body/eval_jaxpr/ppermute | solution.py:24
  207.9 10.2 %collective-permute-start.1 = (f32[4,64,128]{2,1,0:T(8,128)S(1)}, f32[4,64,128]{2,1,0:T(8,128)S(1)}, u32[]{:S(2)}, u32[]{:S(2)}) collective-permute-start(f32[4,64,128]{2,1,0:T(8,128)S(1)} %get-tuple-element.575), channel_id=1, source_target_pairs={{0,8},{8,16},{16,24},{24,32},{32,40},{40,48},{48,56},{56,64},{64,7... | collective-permute-start | bytes 393224 | tf_op jit(solution)/shard_map/while/body/eval_jaxpr/ppermute | solution.py:22
  223.4 11.9 %collective-permute-start = (f32[4,64,128]{2,1,0:T(8,128)S(1)}, f32[4,64,128]{2,1,0:T(8,128)S(1)}, u32[]{:S(2)}, u32[]{:S(2)}) collective-permute-start(f32[4,64,128]{2,1,0:T(8,128)S(1)} %get-tuple-element.574), channel_id=1, source_target_pairs={{8,0},{16,8},{24,16},{32,24},{40,32},{48,40},{56,48},{64,56},{72,6... | collective-permute-start | bytes 393224 | tf_op jit(solution)/shard_map/while/body/eval_jaxpr/ppermute | solution.py:24
  224.7 10.6 %collective-permute-start.1 = (f32[4,64,128]{2,1,0:T(8,128)S(1)}, f32[4,64,128]{2,1,0:T(8,128)S(1)}, u32[]{:S(2)}, u32[]{:S(2)}) collective-permute-start(f32[4,64,128]{2,1,0:T(8,128)S(1)} %get-tuple-element.575), channel_id=1, source_target_pairs={{0,8},{8,16},{16,24},{24,32},{32,40},{40,48},{48,56},{56,64},{64,7... | collective-permute-start | bytes 393224 | tf_op jit(solution)/shard_map/while/body/eval_jaxpr/ppermute | solution.py:22
  240.5 11.9 %collective-permute-start = (f32[4,64,128]{2,1,0:T(8,128)S(1)}, f32[4,64,128]{2,1,0:T(8,128)S(1)}, u32[]{:S(2)}, u32[]{:S(2)}) collective-permute-start(f32[4,64,128]{2,1,0:T(8,128)S(1)} %get-tuple-element.574), channel_id=1, source_target_pairs={{8,0},{16,8},{24,16},{32,24},{40,32},{48,40},{56,48},{64,56},{72,6... | collective-permute-start | bytes 393224 | tf_op jit(solution)/shard_map/while/body/eval_jaxpr/ppermute | solution.py:24
  241.8 10.6 %collective-permute-start.1 = (f32[4,64,128]{2,1,0:T(8,128)S(1)}, f32[4,64,128]{2,1,0:T(8,128)S(1)}, u32[]{:S(2)}, u32[]{:S(2)}) collective-permute-start(f32[4,64,128]{2,1,0:T(8,128)S(1)} %get-tuple-element.575), channel_id=1, source_target_pairs={{0,8},{8,16},{16,24},{24,32},{32,40},{40,48},{48,56},{56,64},{64,7... | collective-permute-start | bytes 393224 | tf_op jit(solution)/shard_map/while/body/eval_jaxpr/ppermute | solution.py:22
  257.6 11.9 %collective-permute-start = (f32[4,64,128]{2,1,0:T(8,128)S(1)}, f32[4,64,128]{2,1,0:T(8,128)S(1)}, u32[]{:S(2)}, u32[]{:S(2)}) collective-permute-start(f32[4,64,128]{2,1,0:T(8,128)S(1)} %get-tuple-element.574), channel_id=1, source_target_pairs={{8,0},{16,8},{24,16},{32,24},{40,32},{48,40},{56,48},{64,56},{72,6... | collective-permute-start | bytes 393224 | tf_op jit(solution)/shard_map/while/body/eval_jaxpr/ppermute | solution.py:24
  258.9 10.6 %collective-permute-start.1 = (f32[4,64,128]{2,1,0:T(8,128)S(1)}, f32[4,64,128]{2,1,0:T(8,128)S(1)}, u32[]{:S(2)}, u32[]{:S(2)}) collective-permute-start(f32[4,64,128]{2,1,0:T(8,128)S(1)} %get-tuple-element.575), channel_id=1, source_target_pairs={{0,8},{8,16},{16,24},{24,32},{32,40},{40,48},{48,56},{56,64},{64,7... | collective-permute-start | bytes 393224 | tf_op jit(solution)/shard_map/while/body/eval_jaxpr/ppermute | solution.py:22
  274.8 11.9 %collective-permute-start = (f32[4,64,128]{2,1,0:T(8,128)S(1)}, f32[4,64,128]{2,1,0:T(8,128)S(1)}, u32[]{:S(2)}, u32[]{:S(2)}) collective-permute-start(f32[4,64,128]{2,1,0:T(8,128)S(1)} %get-tuple-element.574), channel_id=1, source_target_pairs={{8,0},{16,8},{24,16},{32,24},{40,32},{48,40},{56,48},{64,56},{72,6... | collective-permute-start | bytes 393224 | tf_op jit(solution)/shard_map/while/body/eval_jaxpr/ppermute | solution.py:24
  276.1 10.6 %collective-permute-start.1 = (f32[4,64,128]{2,1,0:T(8,128)S(1)}, f32[4,64,128]{2,1,0:T(8,128)S(1)}, u32[]{:S(2)}, u32[]{:S(2)}) collective-permute-start(f32[4,64,128]{2,1,0:T(8,128)S(1)} %get-tuple-element.575), channel_id=1, source_target_pairs={{0,8},{8,16},{16,24},{24,32},{32,40},{40,48},{48,56},{56,64},{64,7... | collective-permute-start | bytes 393224 | tf_op jit(solution)/shard_map/while/body/eval_jaxpr/ppermute | solution.py:22
  (12 other events, 638.1 us)
where the time goes:
time: 442 us; the launch traced here: 440 us
  blocking collectives  117 us (26%)
  starting transfers between devices  102 us (23%)
  waiting for transfers between devices  65.9 us (15%)
  other arithmetic  59.3 us (13%)
  local copies, waits for them, and re-layouts  57.9 us (13%)
  matrix products  34.9 us (8%)
    psum x3, blocking collectives, over_axes(): x = lax.psum(x, axis)  80 us
    ppermute x17, starting transfers between devices, extended(): lax.ppermute(tail, axis, [(i, (i + 1) % count) for i in range(ends)])  79.8 us
    ppermute x17, waiting for transfers between devices, extended(): lax.ppermute(tail, axis, [(i, (i + 1) % count) for i in range(ends)])  65.9 us
    add x16, other arithmetic, advance(): 2.0 * present - earlier + courant * stencil(padded, present)  39.2 us
    all_gather x1, blocking collectives, turned_gather(): result = lax.all_gather(both, axis, axis=0, tiled=True)  36.9 us
    gather x16, local copies, waits for them, and re-layouts, advance(): recorded = jnp.where(inside, surface[safe_index], 0.0)  31.1 us
    ppermute x17, starting transfers between devices, extended(): lax.ppermute(head, axis, [((i + 1) % count, i) for i in range(ends)])  22 us
    dot_general x8, matrix products, forward(): jnp.dot(tile, plane, preferred_element_type=jnp.float32)  17.5 us
  transfers between devices with their start and end apart: 34, of which 16 were waited for; matrix products, arithmetic and copies ran while one was open for 34% of the time, Pallas kernels for 0%

commit v1 on v0

v1 whole, which is shorter than its diff:
```python
import functools

import jax
import jax.numpy as jnp
from jax import lax
from jax.experimental import pallas as pl
from jax.experimental.pallas import tpu as pltpu
from jax.sharding import Mesh
from jax.sharding import PartitionSpec as P

MP = ("x", "z", "y_lo")
STATION = ("station_hi", "core")
MESH = MP + STATION


STENCIL = (-205.0 / 72.0, 8.0 / 5.0, -1.0 / 5.0, 8.0 / 315.0, -1.0 / 560.0)
TIME_RATIO = 0.1
SPLIT = (4, 12, 2)


def extended(cells, sides, width):
    for axis, dim in sides:
        count = lax.axis_size(axis)
        ends = count - 1
        head = lax.slice_in_dim(cells, 0, width, axis=dim)
        tail = lax.slice_in_dim(cells, cells.shape[dim] - width, cells.shape[dim], axis=dim)
        cells = jnp.concatenate(
            [
                lax.ppermute(tail, axis, [(i, (i + 1) % count) for i in range(ends)]),
                cells,
                lax.ppermute(head, axis, [((i + 1) % count, i) for i in range(ends)]),
            ],
            axis=dim,
        )
    return cells


def over_axes(x, axes):
    for axis in axes:
        x = lax.psum(x, axis)
    return x


def turned_gather(arrays, axis, dims):
    turned = [jnp.moveaxis(a, dim, 0) for a, dim in zip(arrays, dims)]
    widths = [t[0].size for t in turned]
    both = jnp.concatenate([t.reshape(-1, w) for t, w in zip(turned, widths)], axis=1)
    result = lax.all_gather(both, axis, axis=0, tiled=True)
    blocks = jnp.split(result, [sum(widths[:k]) for k in range(1, len(widths))], axis=1)
    return tuple(
        (
            jnp.moveaxis(b.reshape(-1, *t.shape[1:]), 0, dim)
            for b, t, dim in zip(blocks, turned, dims)
        )
    )


MESH_ID = pl.DeviceIdType.MESH
SIDES = ((-1, 0), (1, 0), (0, -1), (0, 1), (-1, -1), (-1, 1), (1, -1), (1, 1))
ROW0 = 16
PLANE0 = 8


def place():
    x, z, low, high, core = (lax.axis_index(axis) for axis in MESH)
    nz = lax.axis_size("z")
    slab = (x * nz + z) * 2 + core
    return slab, high * 2 + low, low, core


def device_at(slab, block):
    nz = lax.axis_size("z")
    column = slab // 2
    return (column // nz, lax.rem(column, nz), lax.rem(block, 2), block // 2, lax.rem(slab, 2))


def advance(ref, prev, courant, mask, pulse, zmask, p0, planes, r0):
    rows = pl.ds(r0, 8)
    here = ref[pl.ds(p0, planes), rows, :]
    lap = 3.0 * STENCIL[0] * here
    for d in range(1, 5):
        pairs = ref[pl.ds(p0 + d, planes), rows, :] + ref[pl.ds(p0 - d, planes), rows, :]
        pairs = pairs + ref[pl.ds(p0, planes), pl.ds(r0 + d, 8), :]
        pairs = pairs + ref[pl.ds(p0, planes), pl.ds(r0 - d, 8), :]
        lap = lap + STENCIL[d] * pairs
        lap = lap + pltpu.roll(here, d, 2) * zmask[2 * d - 2][None]
        lap = lap + pltpu.roll(here, here.shape[2] - d, 2) * zmask[2 * d - 1][None]
    at = (pl.ds(p0, planes), rows)
    return 2.0 * here - prev[at] + courant[at] * lap + pulse * mask[at]


def wave_kernel(
    p_now, p_prev, velocity, wavelet, source, receivers, field, traces,
    w, v, courant, mask, zmask, hits,
    init_send, init_recv, halo_send, halo_recv, tail_send, tail_recv,
):
    slab, block, low, core = place()
    slabs = lax.axis_size(MP)
    blocks = lax.axis_size("station_hi") * 2
    lateral, vertical = p_now.shape[1:]
    same = core == low
    inner = 1 - 2 * core
    outer = -inner
    pair = 1 - 2 * low

    def there(ds, db):
        return (slab + ds >= 0) & (slab + ds < slabs) & (block + db >= 0) & (block + db < blocks)

    def window(b):
        start = jnp.clip(8 * (b - 1), 0, lateral - 24)
        return pl.multiple_of(start, 8), pl.multiple_of(ROW0 + start - 8 * b, 8)

    zero = jnp.zeros((24, 24, vertical), jnp.float32)
    for ref in (w.at[0], w.at[1], v, courant):
        ref[:, pl.ds(8, 24), :] = zero

    barrier = pltpu.get_barrier_semaphore()
    for other in range(2 * blocks):
        b, k = other // 2, other % 2

        @pl.when((b != block) | (k != core))
        def _():
            pl.semaphore_signal(
                barrier, 1, device_id=device_at(slab - core + k, b), device_id_type=MESH_ID
            )

    for db in (-1, 0, 1):

        @pl.when(there(outer, db))
        def _():
            pl.semaphore_signal(
                barrier, 1, device_id=device_at(slab + outer, block + db), device_id_type=MESH_ID
            )

    crossing = sum(jnp.where(there(outer, db), 1, 0) for db in (-1, 0, 1))
    pl.semaphore_wait(barrier, 2 * blocks - 1 + crossing)

    arrays = (p_now, p_prev, velocity)
    places = (w.at[0], v, courant)

    def own_package(b, target, k):
        start, to = window(b)
        return [
            pltpu.make_async_remote_copy(
                a.at[:, pl.ds(start, 24), :],
                p.at[pl.ds(PLANE0, 8), pl.ds(to, 24), :],
                init_send.at[k, n], init_recv.at[0, n], device_id=target, device_id_type=MESH_ID,
            )
            for n, (a, p) in enumerate(zip(arrays, places))
        ]

    def halo_package(b, side, target, k, landing):
        start, to = window(b)
        left = side < 0
        near_from = jnp.where(left, 4, 0)
        near_to = jnp.where(left, 4, 16)
        rows = pl.multiple_of(8 * b, 8)
        copies = [
            pltpu.make_async_remote_copy(
                p_now.at[:, pl.ds(start, 24), :],
                w.at[0, pl.ds(jnp.where(left, 0, 16), 8), pl.ds(to, 24), :],
                init_send.at[k, 0], init_recv.at[landing, 0],
                device_id=target, device_id_type=MESH_ID,
            )
        ]
        for n in (1, 2):
            copies.append(
                pltpu.make_async_remote_copy(
                    arrays[n].at[pl.ds(near_from, 4), pl.ds(rows, 8), :],
                    places[n].at[pl.ds(near_to, 4), pl.ds(ROW0, 8), :],
                    init_send.at[k, n], init_recv.at[landing, n],
                    device_id=target, device_id_type=MESH_ID,
                )
            )
        return copies

    paired = block + pair
    partner = device_at(slab, paired)

    @pl.when(same)
    def _():
        for copy in own_package(paired, partner, 0):
            copy.start()
        for k, b in ((1, block), (2, paired)):

            @pl.when(there(outer, 0))
            def _():
                for copy in halo_package(b, -outer, device_at(slab + outer, b), k, 2):
                    copy.start()

    @pl.when(jnp.logical_not(same))
    def _():
        for copy in halo_package(paired, inner, partner, 0, 1):
            copy.start()

    start, to = window(block)
    rows = pl.multiple_of(8 * block, 8)

    @pl.when(same)
    def _():
        for a, p in zip(arrays, places):
            p[pl.ds(PLANE0, 8), pl.ds(to, 24), :] = a[:, pl.ds(start, 24), :]

    @pl.when(jnp.logical_not(same))
    def _():
        left = inner < 0
        w[0, pl.ds(jnp.where(left, 0, 16), 8), pl.ds(to, 24), :] = p_now[:, pl.ds(start, 24), :]
        for a, p in ((p_prev, v), (velocity, courant)):
            p[pl.ds(jnp.where(left, 4, 16), 4), pl.ds(ROW0, 8), :] = a[
                pl.ds(jnp.where(left, 4, 0), 4), pl.ds(rows, 8), :
            ]

    source_cell = source[0]
    source_z = lax.rem(source_cell, vertical)
    source_xy = source_cell // vertical
    source_y = lax.rem(source_xy, lateral)
    source_x = source_xy // lateral
    shape = (24, 24, vertical)
    at_x = lax.broadcasted_iota(jnp.int32, shape, 0) + (8 * slab - PLANE0)
    at_y = lax.broadcasted_iota(jnp.int32, shape, 1) + (8 * block + 8 - ROW0)
    at_z = lax.broadcasted_iota(jnp.int32, shape, 2)
    hit = (at_x == source_x) & (at_y == source_y) & (at_z == source_z)
    mask[:, pl.ds(8, 24), :] = jnp.where(hit, 1.0, 0.0)
    lane = lax.broadcasted_iota(jnp.int32, (8, vertical), 1)
    for d in range(1, 5):
        zmask[2 * d - 2] = jnp.where(lane >= d, STENCIL[d], 0.0)
        zmask[2 * d - 1] = jnp.where(lane < vertical - d, STENCIL[d], 0.0)
    nrec = receivers.shape[1]
    cell = (8 * slab + lax.broadcasted_iota(jnp.int32, (8, 8, nrec), 0)) * lateral + (
        8 * block + lax.broadcasted_iota(jnp.int32, (8, 8, nrec), 1)
    )
    hits[...] = jnp.where(cell == receivers[...][None], 1.0, 0.0)

    @pl.when(same)
    def _():
        for copy in own_package(paired, partner, 0):
            copy.wait_send()
        for k, b in ((1, block), (2, paired)):

            @pl.when(there(outer, 0))
            def _():
                for copy in halo_package(b, -outer, device_at(slab + outer, b), k, 2):
                    copy.wait_send()

        for copy in halo_package(block, inner, partner, 0, 1):
            copy.wait_recv()

    @pl.when(jnp.logical_not(same))
    def _():
        for copy in halo_package(paired, inner, partner, 0, 1):
            copy.wait_send()
        for copy in own_package(block, partner, 0):
            copy.wait_recv()

    @pl.when(there(outer, 0))
    def _():
        for copy in halo_package(block, outer, partner, 0, 2):
            copy.wait_recv()

    scaled = TIME_RATIO * courant[:, pl.ds(8, 24), :]
    courant[:, pl.ds(8, 24), :] = scaled * scaled

    def region(ds, db, near):
        plane = PLANE0 + 8 * ds
        count = 8
        if near and ds:
            plane, count = (4, 4) if ds < 0 else (16, 4)
        return pl.ds(plane, count), pl.ds(ROW0 + 8 * db, 8)

    def halo(slot, k):
        ds, db = SIDES[k]
        corner = ds != 0 and db != 0
        to = region(-ds, -db, corner)
        if corner:
            begin = (PLANE0, ROW0)[0] + (4 if ds > 0 else 0)
            source_at = (pl.ds(begin, 4), pl.ds(ROW0, 8))
        else:
            source_at = (pl.ds(PLANE0, 8), pl.ds(ROW0, 8))
        opposite = SIDES.index((-ds, -db))
        return pltpu.make_async_remote_copy(
            w.at[(slot, *source_at)], w.at[(slot, *to)],
            halo_send.at[k], halo_recv.at[slot, opposite],
            device_id=device_at(slab + ds, block + db), device_id_type=MESH_ID,
        )

    def arriving(slot, k):
        ds, db = SIDES[k]
        corner = ds != 0 and db != 0
        at = region(ds, db, corner)
        return pltpu.make_async_remote_copy(
            w.at[(slot, *at)], w.at[(slot, *at)],
            halo_send.at[k], halo_recv.at[slot, k],
            device_id=device_at(slab + ds, block + db), device_id_type=MESH_ID,
        )

    own = (pl.ds(PLANE0, 8), pl.ds(ROW0, 8))

    def record(values, n):
        top = jnp.broadcast_to(values[:, :, 0:1], values.shape)
        for half in range(nrec // 128):
            part = jnp.sum(top * hits[:, :, half * 128 : (half + 1) * 128], axis=0)
            row = n * (nrec // 128) + half
            traces[pl.ds(row, 1), :] = jnp.sum(part, axis=0, keepdims=True)

    def first(slot, m):
        pulse = wavelet[2 * m]
        here = w.at[slot]
        for p0 in (4, 16):
            new = advance(here, v, courant, mask, pulse, zmask, p0, 4, ROW0)
            v[pl.ds(p0, 4), pl.ds(ROW0, 8), :] = new
        for p0 in range(8, 16, 2):
            for r0 in (12, 20):
                new = advance(here, v, courant, mask, pulse, zmask, p0, 2, r0)
                v[pl.ds(p0, 2), pl.ds(r0, 8), :] = new

    def second(slot, m, target):
        pulse = wavelet[2 * m + 1]
        for p0 in range(8, 16, 2):
            new = advance(v, w.at[slot], courant, mask, pulse, zmask, p0, 2, ROW0)
            target[pl.ds(p0, 2), pl.ds(ROW0, 8), :] = new

    pairs = wavelet.shape[0] // 2

    def body(m, unused):
        slot = lax.rem(m, 2)
        later = 1 - slot
        first(slot, m)
        second(slot, m, w.at[later])
        for k, (ds, db) in enumerate(SIDES):

            @pl.when(there(ds, db))
            def _():
                halo(later, k).start()

        record(v[own], 2 * m)
        record(w[(later, *own)], 2 * m + 1)
        for k, (ds, db) in enumerate(SIDES):

            @pl.when(there(ds, db))
            def _():
                halo(later, k).wait_send()
                arriving(later, k).wait_recv()

        return unused

    lax.fori_loop(0, pairs - 1, body, 0)
    slot = (pairs - 1) % 2
    first(slot, pairs - 1)
    second(slot, pairs - 1, w.at[1 - slot])
    last = w.at[1 - slot]

    def handing(high, k):
        return pltpu.make_async_remote_copy(
            last.at[own], field.at[:, pl.ds(rows, 8), :],
            tail_send.at[high, k], tail_recv.at[block],
            device_id=(*device_at(slab, 2 * high + core)[:4], k), device_id_type=MESH_ID,
        )

    for high in range(blocks // 2):
        for k in range(2):

            @pl.when((2 * high + core != block) | (k != core))
            def _():
                handing(high, k).start()

    @pl.when(same)
    def _():
        field[:, pl.ds(rows, 8), :] = last[own]

    record(v[own], 2 * pairs - 2)
    record(last[own], 2 * pairs - 1)
    for high in range(blocks // 2):
        for k in range(2):

            @pl.when((2 * high + core != block) | (k != core))
            def _():
                handing(high, k).wait_send()

    for b in range(blocks):

        @pl.when((b != block) | jnp.logical_not(same))
        def _():
            pltpu.make_async_remote_copy(
                last.at[own], field.at[:, pl.ds(8 * b, 8), :],
                tail_send.at[0, 0], tail_recv.at[b],
                device_id=partner, device_id_type=MESH_ID,
            ).wait_recv()


def wave(p_now, p_prev, velocity, wavelet, source_cell, receiver_cells):
    vertical = p_now.shape[2]
    nrec = receiver_cells.shape[0]
    blocks = lax.axis_size("station_hi") * 2
    f32 = jnp.float32
    padded = (24, 40, vertical)
    vmem, smem = (pl.BlockSpec(memory_space=space) for space in (pltpu.VMEM, pltpu.SMEM))
    dma = pltpu.SemaphoreType.DMA
    return pl.pallas_call(
        wave_kernel,
        out_shape=(
            jax.ShapeDtypeStruct(p_now.shape, f32),
            jax.ShapeDtypeStruct((wavelet.shape[0] * nrec // 128, 128), f32),
        ),
        in_specs=[vmem, vmem, vmem, smem, smem, vmem],
        out_specs=(vmem, vmem),
        scratch_shapes=[
            pltpu.VMEM((2, *padded), f32),
            pltpu.VMEM(padded, f32),
            pltpu.VMEM(padded, f32),
            pltpu.VMEM(padded, f32),
            pltpu.VMEM((8, 8, vertical), f32),
            pltpu.VMEM((8, 8, nrec), f32),
            dma((3, 3)), dma((3, 3)), dma((8,)), dma((2, 8)), dma((blocks // 2, 2)), dma((blocks,)),
        ],
        compiler_params=pltpu.CompilerParams(
            collective_id=0, has_side_effects=True, vmem_limit_bytes=32 * 2**20
        ),
    )(p_now, p_prev, velocity, wavelet, source_cell, receiver_cells.reshape(1, -1))


def kernel_tile(plane_x, station_x, station_y, cell_y, cell_z):
    delta_x = plane_x - station_x
    delta_y = cell_y[None, :] - station_y[:, None]
    radius_sq = (
        delta_x[:, None] * delta_x[:, None] + delta_y * delta_y + cell_z[None, :] * cell_z[None, :]
    )
    return (cell_z[None, :] / (radius_sq * jnp.sqrt(radius_sq))).astype(jnp.bfloat16)


def cross_terms(padded, slab, lateral, vertical):
    diff_x = (
        padded[:, 2 : 2 + slab, 1 : 1 + lateral, 1 : 1 + vertical]
        - padded[:, 0:slab, 1 : 1 + lateral, 1 : 1 + vertical]
    ) * 0.5
    diff_y = (
        padded[:, 1 : 1 + slab, 2 : 2 + lateral, 1 : 1 + vertical]
        - padded[:, 1 : 1 + slab, 0:lateral, 1 : 1 + vertical]
    ) * 0.5
    diff_z = (
        padded[:, 1 : 1 + slab, 1 : 1 + lateral, 2 : 2 + vertical]
        - padded[:, 1 : 1 + slab, 1 : 1 + lateral, 0:vertical]
    ) * 0.5
    first = diff_y[0] * diff_z[1] - diff_z[0] * diff_y[1]
    second = diff_z[0] * diff_x[1] - diff_x[0] * diff_z[1]
    third = diff_x[0] * diff_y[1] - diff_y[0] * diff_x[1]
    return jnp.stack([first, second, third])


def per_device(
    p_now, p_prev, velocity, density, wavelet, source_cell, receiver_cells, station_cells, observed
):
    slab, lateral, vertical = p_now.shape
    offset_x = lax.axis_index(MP) * slab
    offset_y = 0
    global_x = offset_x + jnp.arange(slab, dtype=jnp.int32)
    global_y = offset_y + jnp.arange(lateral, dtype=jnp.int32)
    last_field, traces = wave(p_now, p_prev, velocity, wavelet, source_cell, receiver_cells)
    traces = lax.psum(traces, MESH).reshape(-1, receiver_cells.shape[0])
    stacked = jnp.stack([velocity, density])
    padded_model = extended(stacked, ((MP, 1),), 1)
    padded_model = jnp.pad(padded_model, ((0, 0), (0, 0), (1, 1), (1, 1)))
    cross_gradient = cross_terms(padded_model, slab, lateral, vertical)
    station_x = (station_cells // lateral).astype(jnp.float32)
    station_y = (station_cells % lateral).astype(jnp.float32)
    cell_y = (jnp.arange(lateral * vertical, dtype=jnp.int32) // vertical).astype(jnp.float32)
    cell_z = (jnp.arange(lateral * vertical, dtype=jnp.int32) % vertical).astype(jnp.float32) + 1.0
    planes = density.astype(jnp.bfloat16).reshape(slab, lateral * vertical)
    plane_xs = global_x.astype(jnp.float32)

    def forward(totals, packed):
        plane_x, plane = packed
        tile = kernel_tile(plane_x, station_x, station_y, cell_y, cell_z)
        return (totals + jnp.dot(tile, plane, preferred_element_type=jnp.float32), None)

    partial_value, unused_out = lax.scan(
        forward, jnp.zeros((station_cells.shape[0],), jnp.float32), (plane_xs, planes)
    )
    predicted = over_axes(partial_value, MP)
    gravity_residual = predicted - observed
    share_rows = lateral // lax.axis_size(STATION)
    every_residual, every_x, every_y = turned_gather(
        (gravity_residual, station_x, station_y), STATION, (0, 0, 0)
    )
    every_low = every_residual.astype(jnp.bfloat16)
    share_index = jnp.arange(share_rows * vertical, dtype=jnp.int32)
    share_y = (lax.axis_index(STATION) * share_rows + share_index // vertical).astype(jnp.float32)
    share_z = (share_index % vertical).astype(jnp.float32) + 1.0

    def adjoint_rows(plane_x):
        tile = kernel_tile(plane_x, every_x, every_y, share_y, share_z)
        return jnp.dot(every_low, tile, preferred_element_type=jnp.float32)

    density_gradient = lax.map(adjoint_rows, plane_xs).reshape(slab, share_rows, vertical)
    return (last_field, traces, gravity_residual, density_gradient, cross_gradient)


def solution(mesh):
    split = Mesh(
        mesh.devices.reshape(*SPLIT, mesh.shape["station"] // 2, 2), MESH
    )
    slabs = P(MP, None, None)
    return jax.shard_map(
        per_device,
        mesh=split,
        in_specs=(slabs, slabs, slabs, slabs, P(), P(), P(), P(STATION), P(STATION)),
        out_specs=(slabs, P(), P(STATION), P(MP, STATION, None), P(None, MP, None, None)),
        check_vma=False,
    )
```

time: 442 us -> 299 us (0.68)
  starting transfers between devices: 102 us -> 5.33 us
  waiting for transfers between devices: 65.9 us -> 0.01 us
  blocking collectives: 117 us -> 180 us
  Pallas kernels: 0 us -> 48.8 us
  local copies, waits for them, and re-layouts: 57.9 us -> 11.6 us
  other arithmetic: 59.3 us -> 15.6 us
    psum x0 -> x1, blocking collectives: none -> 112 us  [per_device(): traces = lax.psum(traces, MESH).reshape(-1, receiver_cells.shape[0])]
    ppermute x17 -> x1, starting transfers between devices: 79.8 us -> 4.03 us  [extended(): lax.ppermute(tail, axis, [(i, (i + 1) % count) for i in range(ends)])]
    ppermute x17 -> x1, waiting for transfers between devices: 65.9 us -> 0.01 us  [extended(): lax.ppermute(tail, axis, [(i, (i + 1) % count) for i in range(ends)])]
    pallas_call x0 -> x1, Pallas kernels: none -> 48.8 us  [wave(): pl.pallas_call(wave_kernel, out_shape=(jax.ShapeDtypeStruct(p_now.shape,...]
    add x16 -> x0, other arithmetic: 39.2 us -> none  [advance(): 2.0 * present - earlier + courant * stencil(padded, present)]
    psum x3, blocking collectives: 80 us -> 41.9 us  [over_axes(): x = lax.psum(x, axis)]
    gather x16 -> x0, local copies, waits for them, and re-layouts: 31.1 us -> none  [advance(): recorded = jnp.where(inside, surface[safe_index], 0.0)]
    ppermute x17 -> x1, starting transfers between devices: 22 us -> 1.29 us  [extended(): lax.ppermute(head, axis, [((i + 1) % count, i) for i in range(ends)])]
  transfers between devices with their start and end apart: 34 -> 2, of which waited for: 16 -> 0; matrix products, arithmetic and copies ran while one was open for 34% -> 20% of each run, Pallas kernels for 0% -> 16%
where the time goes in v1:
time: 299 us; the launch traced here: 298 us
  blocking collectives  180 us (60%)
  Pallas kernels  48.8 us (16%)
  matrix products  34.8 us (12%)
  other arithmetic  15.6 us (5%)
  local copies, waits for them, and re-layouts  11.6 us (4%)
  starting transfers between devices  5.33 us (2%)
    psum x1, blocking collectives, per_device(): traces = lax.psum(traces, MESH).reshape(-1, receiver_cells.shape[0])  112 us
    pallas_call x1, Pallas kernels, wave(): pl.pallas_call(wave_kernel, out_shape=(jax.ShapeDtypeStruct(p_now.shape,...  48.8 us
    psum x3, blocking collectives, over_axes(): x = lax.psum(x, axis)  41.9 us
    all_gather x1, blocking collectives, turned_gather(): result = lax.all_gather(both, axis, axis=0, tiled=True)  26.3 us
    dot_general x8, matrix products, forward(): jnp.dot(tile, plane, preferred_element_type=jnp.float32)  17.5 us
    dot_general x8, matrix products, adjoint_rows(): return jnp.dot(every_low, tile, preferred_element_type=jnp.float32)  17.3 us
    dynamic_slice x16, local copies, waits for them, and re-layouts, per_device(): lax.scan(forward, jnp.zeros((station_cells.shape[0],), jnp.float32), (pla...  9.42 us
  transfers between devices with their start and end apart: 2, of which 0 were waited for; matrix products, arithmetic and copies ran while one was open for 20% of the time, Pallas kernels for 16%

profile of v1, /device:TPU:1, one launch (start us, length us, event | category | flops | bytes accessed | tf_op | source)
XLA Modules:
  0.0 298.2 jit_solution(15350539075855808890)
XLA Ops:
  0.6 0.8 pad_maximum_fusion.5
  1.5 4.0 %collective-permute-start = (f32[2,1,64,128]{3,2,1,0:T(8,128)S(1)}, f32[2,1,64,128]{3,2,1,0:T(8,128)S(1)}, u32[]{:S(2)}, u32[]{:S(2)}) collective-permute-start(f32[2,1,64,128]{3,2,1,0:T(8,128)S(1)} %get-tuple-element.249), channel_id=1, source_target_pairs={{0,8},{8,16},{16,24},{24,32},{32,40},{40,48},{48,56},{56,64},{64,7... | collective-permute-start | bytes 196616 | tf_op jit(solution)/shard_map/ppermute | solution.py:29
  5.5 1.3 collective-permute-start.1
  6.8 1.0 convert_bitcast_fusion
  7.8 0.7 fusion.60
  8.6 28.2 %while.25 = (s32[]{:T(128)}, f32[128]{0:T(128)S(1)}, f32[8]{0:T(128)S(1)}, f32[128]{0:T(128)S(1)}, f32[128]{0:T(128)S(1)}, /*index=5*/bf16[8,8192]{1,0:T(8,128)(2,1)S(1)}, s32[]{:T(128)}, s32[]{:T(128)}) while((s32[]{:T(128)}, f32[128]{0:T(128)S(1)}, f32[8]{0:T(128)S(1)}, f32[128]{0:T(128)S(1)}, f32[128]{0:T(128)S(1)}, ...), condition=%wide.region_2.3_spmd.clone, body=%wide.region_1.2_spmd.clone.sunk | while | flops 9650691 | bytes 232563 | solution.py:475
  9.9 2.2 fusion.87
  13.5 2.2 fusion.87
  17.0 2.2 fusion.87
  20.5 2.2 fusion.87
  24.0 2.2 fusion.87
  27.6 2.2 fusion.87
  31.1 2.2 fusion.87
  34.6 2.2 fusion.87
  36.8 21.5 %psum.29 = f32[128]{0:T(128)S(1)} all-reduce(f32[128]{0:T(128)S(1)} %get-tuple-element.167), channel_id=1, replica_groups=mesh['x'=4,'z'=12,'y_lo'=2,'station_hi'=4,'core'=2] {'x'}, use_global_device_ids=true, to_apply=%region_3.4 | all-reduce | flops 128 | bytes 1024 | tf_op jit(solution)/shard_map/psum | solution.py:40
  58.3 16.7 %psum.30 = f32[128]{0:T(128)S(1)} all-reduce(f32[128]{0:T(128)S(1)} %psum.29), channel_id=1, replica_groups=mesh['x'=4,'z'=12,'y_lo'=2,'station_hi'=4,'core'=2] {'z'}, use_global_device_ids=true, to_apply=%region_4.5 | all-reduce | flops 128 | bytes 1024 | tf_op jit(solution)/shard_map/psum | solution.py:40
  74.9 3.8 %psum.31 = f32[128]{0:T(128)S(1)} all-reduce(f32[128]{0:T(128)S(1)} %psum.30), channel_id=1, replica_groups=mesh['x'=4,'z'=12,'y_lo'=2,'station_hi'=4,'core'=2] {'y_lo'}, use_global_device_ids=true, to_apply=%region_5.6 | all-reduce | flops 128 | bytes 1024 | tf_op jit(solution)/shard_map/psum | solution.py:40
  78.7 26.3 %all_gather.3 = f32[1024,3]{0,1:T(4,128)S(1)} all-gather(f32[128,3]{0,1:T(4,128)S(1)} %pad_maximum_fusion.7), channel_id=1, replica_groups=mesh['x'=4,'z'=12,'y_lo'=2,'station_hi'=4,'core'=2] {'station_hi','core'}, dimensions={0}, use_global_device_ids=true | all-gather | bytes 13824 | tf_op jit(solution)/shard_map/all_gather | solution.py:48
  105.2 28.4 %while.24 = (s32[]{:T(128)}, f32[8,1024]{1,0:T(8,128)S(1)}, f32[8]{0:T(128)S(1)}, f32[1024]{0:T(1024)S(1)}, f32[1024,1]{0,1:T(1,128)S(1)}, /*index=5*/bf16[1024]...) while((s32[]{:T(128)}, f32[8,1024]{1,0:T(8,128)S(1)}, f32[8]{0:T(128)S(1)}, f32[1024]{0:T(1024)S(1)}, ...), condition=%wide.region_7.8_spmd.clone, body=%wide.region_6.7_spmd.clone.sunk | while | flops 9466882 | bytes 59509 | solution.py:493
  105.8 0.6 fusion.80
  106.5 2.2 fusion.81
  110.1 2.2 fusion.81
  113.6 2.2 fusion.81
  117.2 2.2 fusion.81
  120.7 2.2 fusion.81
  124.3 2.2 fusion.81
  127.8 2.2 fusion.81
  131.4 2.2 fusion.81
  135.0 48.8 %shard_map.128 = (f32[8,64,128]{2,1,0:T(8,128)S(1)}, f32[32,128]{1,0:T(8,128)S(1)}) custom-call(f32[8,64,128]{2,1,0:T(8,128)S(1)} %copy-done.1, f32[8,64,128]{2,1,0:T(8,128)S(1)} %copy-done.2, f32[8,64,128]{2,1,0:T(8,128)S(1)} %copy-done, f32[16]{0:T(128)S(1)} %copy-done.4, s32[1]{0:T(128)S(6)} %copy.34.source, s32[1,256]{1,0:T(1,128)S(1)} %bitcast.49), custom_call_target="tpu_custom_call" | custom-call | tf_op jit(solution)/shard_map/pallas_call | solution.py:398
  183.8 111.6 %psum.28 = f32[16,256]{1,0:T(8,128)} all-reduce(f32[16,256]{1,0:T(8,128)S(1)} %reshape.106), channel_id=1, replica_groups=mesh['x'=4,'z'=12,'y_lo'=2,'station_hi'=4,'core'=2] {'x','z','y_lo','sta..., use_global_device_ids=true, to_apply=%region_0.0 | all-reduce | flops 4096 | bytes 32768 | tf_op jit(solution)/shard_map/psum | solution.py:458
  296.5 1.0 pad_maximum_fusion
  297.5 0.7 copy.35
  (119 shorter events, 22.4 us)
Async XLA Ops:
  1.5 293.9 %collective-permute-start = (f32[2,1,64,128]{3,2,1,0:T(8,128)S(1)}, f32[2,1,64,128]{3,2,1,0:T(8,128)S(1)}, u32[]{:S(2)}, u32[]{:S(2)}) collective-permute-start(f32[2,1,64,128]{3,2,1,0:T(8,128)S(1)} %get-tuple-element.249), channel_id=1, source_target_pairs={{0,8},{8,16},{16,24},{24,32},{32,40},{40,48},{48,56},{56,64},{64,7... | collective-permute-start | bytes 196616 | tf_op jit(solution)/shard_map/ppermute | solution.py:29
  5.5 289.9 %collective-permute-start.1 = (f32[2,1,64,128]{3,2,1,0:T(8,128)S(1)}, f32[2,1,64,128]{3,2,1,0:T(8,128)S(1)}, u32[]{:S(2)}, u32[]{:S(2)}) collective-permute-start(f32[2,1,64,128]{3,2,1,0:T(8,128)S(1)} %get-tuple-element.248), channel_id=1, source_target_pairs={{8,0},{16,8},{24,16},{32,24},{40,32},{48,40},{56,48},{64,56},{72,6... | collective-permute-start | bytes 196616 | tf_op jit(solution)/shard_map/ppermute | solution.py:31
  8.6 70.1 %copy-start.7 = (f32[128]{0:T(128)S(1)}, f32[128]{0:T(128)}, u32[]{:S(2)}) copy-start(f32[128]{0:T(128)} %param.21) | copy-start | bytes 1540
  78.7 26.5 %copy-start.6 = (f32[128]{0:T(128)}, f32[128]{0:T(128)S(1)}, u32[]{:S(2)}) copy-start(f32[128]{0:T(128)S(1)} %sub.101) | copy-start | bytes 1540
  105.1 29.8 %copy-start = (f32[8,64,128]{2,1,0:T(8,128)S(1)}, f32[8,64,128]{2,1,0:T(8,128)}, u32[]{:S(2)}) copy-start(f32[8,64,128]{2,1,0:T(8,128)} %velocity.1) | copy-start | bytes 786436
  105.1 29.8 %copy-start.1 = (f32[8,64,128]{2,1,0:T(8,128)S(1)}, f32[8,64,128]{2,1,0:T(8,128)}, u32[]{:S(2)}) copy-start(f32[8,64,128]{2,1,0:T(8,128)} %p_now.1) | copy-start | bytes 786436
  105.1 29.8 %copy-start.2 = (f32[8,64,128]{2,1,0:T(8,128)S(1)}, f32[8,64,128]{2,1,0:T(8,128)}, u32[]{:S(2)}) copy-start(f32[8,64,128]{2,1,0:T(8,128)} %p_prev.1) | copy-start | bytes 786436
  105.2 29.8 %copy-start.3 = (s32[256]{0:T(256)S(1)}, s32[256]{0:T(256)}, u32[]{:S(2)}) copy-start(s32[256]{0:T(256)} %param.19) | copy-start | bytes 3076
  105.2 29.8 %copy-start.4 = (f32[16]{0:T(128)S(1)}, f32[16]{0:T(128)}, u32[]{:S(2)}) copy-start(f32[16]{0:T(128)} %wavelet.1) | copy-start | bytes 196
  105.2 190.2 %copy-start.5 = (f32[8,64,128]{2,1,0:T(8,128)S(1)}, f32[8,64,128]{2,1,0:T(8,128)}, u32[]{:S(2)}) copy-start(f32[8,64,128]{2,1,0:T(8,128)} %param.16) | copy-start | bytes 786436

commit v2 on v1

--- a/solution.py
+++ b/solution.py
@@ -1,5 +1,3 @@
-import functools
-
 import jax
 import jax.numpy as jnp
 from jax import lax
@@ -11,50 +9,9 @@
 MP = ("x", "z", "y_lo")
 STATION = ("station_hi", "core")
 MESH = MP + STATION
-
-
+SPLIT = (4, 12, 2)
 STENCIL = (-205.0 / 72.0, 8.0 / 5.0, -1.0 / 5.0, 8.0 / 315.0, -1.0 / 560.0)
 TIME_RATIO = 0.1
-SPLIT = (4, 12, 2)
-
-
-def extended(cells, sides, width):
-    for axis, dim in sides:
-        count = lax.axis_size(axis)
-        ends = count - 1
-        head = lax.slice_in_dim(cells, 0, width, axis=dim)
-        tail = lax.slice_in_dim(cells, cells.shape[dim] - width, cells.shape[dim], axis=dim)
-        cells = jnp.concatenate(
-            [
-                lax.ppermute(tail, axis, [(i, (i + 1) % count) for i in range(ends)]),
-                cells,
-                lax.ppermute(head, axis, [((i + 1) % count, i) for i in range(ends)]),
-            ],
-            axis=dim,
-        )
-    return cells
-
-
-def over_axes(x, axes):
-    for axis in axes:
-        x = lax.psum(x, axis)
-    return x
-
-
-def turned_gather(arrays, axis, dims):
-    turned = [jnp.moveaxis(a, dim, 0) for a, dim in zip(arrays, dims)]
-    widths = [t[0].size for t in turned]
-    both = jnp.concatenate([t.reshape(-1, w) for t, w in zip(turned, widths)], axis=1)
-    result = lax.all_gather(both, axis, axis=0, tiled=True)
-    blocks = jnp.split(result, [sum(widths[:k]) for k in range(1, len(widths))], axis=1)
-    return tuple(
-        (
-            jnp.moveaxis(b.reshape(-1, *t.shape[1:]), 0, dim)
-            for b, t, dim in zip(blocks, turned, dims)
-        )
-    )
-
-
 MESH_ID = pl.DeviceIdType.MESH
 SIDES = ((-1, 0), (1, 0), (0, -1), (0, 1), (-1, -1), (-1, 1), (1, -1), (1, 1))
 ROW0 = 16
@@ -89,10 +46,21 @@
     return 2.0 * here - prev[at] + courant[at] * lap + pulse * mask[at]
 
 
-def wave_kernel(
-    p_now, p_prev, velocity, wavelet, source, receivers, field, traces,
+def total_of(parts):
+    total = parts[0]
+    for k in range(1, parts.shape[0]):
+        total = total + parts[k]
+    return total
+
+
+def step_kernel(
+    p_now, p_prev, velocity, density, wavelet, source, receivers, cells, observed,
+    field, traces, residual, gradient, crossed,
     w, v, courant, mask, zmask, hits,
     init_send, init_recv, halo_send, halo_recv, tail_send, tail_recv,
+    groups, stations, depth, tiles, sums, low_row, group_send, group_recv,
+    models, model_send, model_recv,
+    record_rows, early_z, early_x, early_y, late_z, late_x, late_y, ring_send, ring_recv,
 ):
     slab, block, low, core = place()
     slabs = lax.axis_size(MP)
@@ -114,6 +82,12 @@
     for ref in (w.at[0], w.at[1], v, courant):
         ref[:, pl.ds(8, 24), :] = zero
 
+    for n in range(2):
+        models[n, 0] = jnp.zeros(models.shape[2:], jnp.float32)
+        models[n, 9] = jnp.zeros(models.shape[2:], jnp.float32)
+        models[n, :, pl.ds(0, 8), :] = jnp.zeros((10, 8, vertical), jnp.float32)
+        models[n, :, pl.ds(8 + lateral, 8), :] = jnp.zeros((10, 8, vertical), jnp.float32)
+
     barrier = pltpu.get_barrier_semaphore()
     for other in range(2 * blocks):
         b, k = other // 2, other % 2
@@ -132,8 +106,59 @@
                 barrier, 1, device_id=device_at(slab + outer, block + db), device_id_type=MESH_ID
             )
 
+    x, z, high = lax.axis_index("x"), lax.axis_index("z"), block // 2
+    nx, nz = lax.axis_size("x"), lax.axis_size("z")
+
+    def on_z(k):
+        return (x, k, low, high, core)
+
+    def on_x(k):
+        return (k // 2, z, low, high, lax.rem(k, 2))
+
+    def on_y(k):
+        return device_at(slab, k)
+
+    me_z, me_x, me_y = z, 2 * x + core, block
+    for d in range(1, nz):
+        pl.semaphore_signal(
+            barrier, 1, device_id=on_z(lax.rem(z + d, nz)), device_id_type=MESH_ID
+        )
+    for d in range(1, nx):
+        for k in range(2):
+            pl.semaphore_signal(
+                barrier, 1, device_id=on_x(2 * lax.rem(x + d, nx) + k), device_id_type=MESH_ID
+            )
+    kept = (x * nz + z) * 2 + low
+    onward = 2 * low - 1
+    beyond = kept + onward
+    more = (beyond >= 0) & (beyond < slabs)
+    far = (beyond // (2 * nz), lax.rem(beyond // 2, nz), 1 - low, high, core)
+
+    @pl.when(more)
+    def _():
+        pl.semaphore_signal(barrier, 1, device_id=far, device_id_type=MESH_ID)
+
     crossing = sum(jnp.where(there(outer, db), 1, 0) for db in (-1, 0, 1))
-    pl.semaphore_wait(barrier, 2 * blocks - 1 + crossing)
+    pl.semaphore_wait(
+        barrier, 2 * blocks - 1 + crossing + nz - 1 + 2 * (nx - 1) + jnp.where(more, 1, 0)
+    )
+
+    own_group = 2 * high + core
+    sizes = (lateral.bit_length() - 1, lateral - 1)
+    groups[own_group, pl.ds(0, 1), :] = (cells[...] >> sizes[0]).astype(jnp.float32)
+    groups[own_group, pl.ds(1, 1), :] = (cells[...] & sizes[1]).astype(jnp.float32)
+    groups[own_group, pl.ds(2, 1), :] = observed[...]
+
+    def group_copy(d, forth):
+        other = lax.rem(own_group + (d if forth else blocks - d), blocks)
+        return pltpu.make_async_remote_copy(
+            groups.at[own_group], groups.at[own_group if forth else other],
+            group_send.at[d], group_recv.at[own_group if forth else other],
+            device_id=(x, z, low, other // 2, lax.rem(other, 2)), device_id_type=MESH_ID,
+        )
+
+    for d in range(1, blocks):
+        group_copy(d, True).start()
 
     arrays = (p_now, p_prev, velocity)
     places = (w.at[0], v, courant)
@@ -196,6 +221,28 @@
     start, to = window(block)
     rows = pl.multiple_of(8 * block, 8)
 
+    def model_copy(n, outward, forth):
+        e = onward if outward else -onward
+        if forth:
+            plane, landing = jnp.where(e > 0, 7, 0), jnp.where(e > 0, 0, 9)
+        else:
+            plane, landing = 0, jnp.where(e > 0, 9, 0)
+        k = 1 if outward else 0
+        return pltpu.make_async_remote_copy(
+            (velocity, density)[n].at[plane], models.at[n, landing, pl.ds(8, lateral), :],
+            model_send.at[n, k], model_recv.at[n, k],
+            device_id=far if outward else partner, device_id_type=MESH_ID,
+        )
+
+    for n in range(2):
+        model_copy(n, False, True).start()
+
+        @pl.when(more)
+        def _():
+            model_copy(n, True, True).start()
+
+        models[n, pl.ds(1, 8), pl.ds(8, lateral), :] = (velocity, density)[n][...]
+
     @pl.when(same)
     def _():
         for a, p in zip(arrays, places):
@@ -231,6 +278,72 @@
     )
     hits[...] = jnp.where(cell == receivers[...][None], 1.0, 0.0)
 
+    step_z = lax.broadcasted_iota(jnp.int32, (vertical, 128), 0).astype(jnp.float32) + 1.0
+    depth[0] = step_z
+    depth[1] = step_z * step_z
+    share = pl.multiple_of(8 * own_group, 8)
+    sums[...] = jnp.zeros(sums.shape, jnp.float32)
+    ngroups = groups.shape[0]
+
+    def forward(q, unused):
+        p, r = q // 4, 2 * lax.rem(q, 4)
+        dx = (8 * kept + p).astype(jnp.float32) - stations[0]
+        dz, dz_sq = depth[0], depth[1]
+        for u in range(2):
+            dy = (share + r + u).astype(jnp.float32) - stations[1]
+            flat = dx * dx + dy * dy
+            for g in range(ngroups):
+                inverse = lax.rsqrt(flat[g : g + 1, :] + dz_sq)
+                tile = (dz * inverse) * (inverse * inverse)
+                tiles[q, pl.ds(u * vertical, vertical), pl.ds(g * 128, 128)] = tile.astype(
+                    jnp.bfloat16
+                )
+        pair = jnp.concatenate(
+            [density[p, pl.ds(share + r, 1), :], density[p, pl.ds(share + r + 1, 1), :]], axis=1
+        )
+        sums[...] += jnp.dot(
+            pair.astype(jnp.bfloat16), tiles[q], preferred_element_type=jnp.float32
+        )
+        return unused
+
+    def adjoint(q, unused):
+        p, r = q // 4, 2 * lax.rem(q, 4)
+        part = lax.dot_general(
+            low_row[...].astype(jnp.bfloat16), tiles[q], (((1,), (1,)), ((), ())),
+            preferred_element_type=jnp.float32,
+        )
+        gradient[p, pl.ds(r, 1), :] = part[:, :vertical]
+        gradient[p, pl.ds(r + 1, 1), :] = part[:, vertical:]
+        return unused
+
+    def cross_plane(p, unused):
+        lanes = lax.broadcasted_iota(jnp.int32, (lateral, vertical), 1)
+
+        def slopes(f):
+            mid = f[p + 1, pl.ds(8, lateral), :]
+            along_x = (f[p + 2, pl.ds(8, lateral), :] - f[p, pl.ds(8, lateral), :]) * 0.5
+            along_y = (f[p + 1, pl.ds(9, lateral), :] - f[p + 1, pl.ds(7, lateral), :]) * 0.5
+            after = jnp.where(lanes < vertical - 1, pltpu.roll(mid, vertical - 1, 1), 0.0)
+            before = jnp.where(lanes > 0, pltpu.roll(mid, 1, 1), 0.0)
+            return along_x, along_y, (after - before) * 0.5
+
+        vx, vy, vz = slopes(models.at[0])
+        qx, qy, qz = slopes(models.at[1])
+        crossed[0, p] = vy * qz - vz * qy
+        crossed[1, p] = vz * qx - vx * qz
+        crossed[2, p] = vx * qy - vy * qx
+        return unused
+
+    for d in range(1, blocks):
+        group_copy(d, True).wait_send()
+        group_copy(d, False).wait_recv()
+    for g in range(ngroups):
+        for n in range(3):
+            stations[n, pl.ds(g, 1), :] = groups[g, pl.ds(n, 1), :]
+    pairs_all = tiles.shape[0]
+    quarter = pairs_all // 4
+    lax.fori_loop(0, quarter, forward, 0)
+
     @pl.when(same)
     def _():
         for copy in own_package(paired, partner, 0):
@@ -300,7 +413,7 @@
         for half in range(nrec // 128):
             part = jnp.sum(top * hits[:, :, half * 128 : (half + 1) * 128], axis=0)
             row = n * (nrec // 128) + half
-            traces[pl.ds(row, 1), :] = jnp.sum(part, axis=0, keepdims=True)
+            record_rows[row // 8, pl.ds(lax.rem(row, 8), 1), :] = jnp.sum(part, axis=0, keepdims=True)
 
     def first(slot, m):
         pulse = wavelet[2 * m]
@@ -321,7 +434,25 @@
 
     pairs = wavelet.shape[0] // 2
 
-    def body(m, unused):
+    def ring(k, buffer, me, n, address, forth, d):
+        other = lax.rem(me + (d if forth else n - d), n)
+        return pltpu.make_async_remote_copy(
+            buffer.at[me], buffer.at[me if forth else other],
+            ring_send.at[k, d], ring_recv.at[k, me if forth else other],
+            device_id=address(other), device_id_type=MESH_ID,
+        )
+
+    def spread(k, buffer, me, address):
+        for d in range(1, buffer.shape[0]):
+            ring(k, buffer, me, buffer.shape[0], address, True, d).start()
+
+    def gathered(k, buffer, me, address):
+        for d in range(1, buffer.shape[0]):
+            ring(k, buffer, me, buffer.shape[0], address, True, d).wait_send()
+            ring(k, buffer, me, buffer.shape[0], address, False, d).wait_recv()
+        return total_of(buffer)
+
+    def step(m, background):
         slot = lax.rem(m, 2)
         later = 1 - slot
         first(slot, m)
@@ -334,6 +465,7 @@
 
         record(v[own], 2 * m)
         record(w[(later, *own)], 2 * m + 1)
+        background()
         for k, (ds, db) in enumerate(SIDES):
 
             @pl.when(there(ds, db))
@@ -341,27 +473,76 @@
                 halo(later, k).wait_send()
                 arriving(later, k).wait_recv()
 
+    def body(m, unused):
+        step(m, lambda: lax.fori_loop(quarter * (m + 1), quarter * (m + 2), forward, 0))
         return unused
 
-    lax.fori_loop(0, pairs - 1, body, 0)
+    lax.fori_loop(0, 3, body, 0)
+
+    def background_3():
+        for g in range(ngroups):
+            early_z[me_z, 0, pl.ds(g, 1), :] = sums[:, pl.ds(g * 128, 128)]
+        early_z[me_z, 1] = record_rows[0]
+        early_z[me_z, 2] = record_rows[1]
+        spread(0, early_z, me_z, on_z)
+        for n in range(2):
+            for outward in (False, True):
+
+                @pl.when(more | (not outward))
+                def _():
+                    model_copy(n, outward, True).wait_send()
+                    model_copy(n, outward, False).wait_recv()
+
+        lax.fori_loop(0, 8, cross_plane, 0)
+
+    def background_4():
+        early_x[me_x] = gathered(0, early_z, me_z, on_z)
+        spread(1, early_x, me_x, on_x)
+
+    def background_5():
+        early_y[me_y] = gathered(1, early_x, me_x, on_x)
+        spread(2, early_y, me_y, on_y)
+
+    def put_traces(rows_at, first_step):
+        for n in range(4):
+            for half in range(2):
+                traces[pl.ds(first_step + n, 1), pl.ds(128 * half, 128)] = rows_at[
+                    2 * n + half : 2 * n + half + 1, :
+                ]
+
+    def background_6():
+        total = gathered(2, early_y, me_y, on_y)
+        left_over = total[0, :ngroups] - stations[2]
+        stations[0] = left_over
+        residual[...] = stations[0, pl.ds(own_group, 1), :]
+        for g in range(ngroups):
+            low_row[:, pl.ds(g * 128, 128)] = left_over[g : g + 1, :]
+        put_traces(total[1], 0)
+        put_traces(total[2], 4)
+        lax.fori_loop(0, pairs_all, adjoint, 0)
+
+    step(3, background_3)
+    step(4, background_4)
+    step(5, background_5)
+    step(6, background_6)
     slot = (pairs - 1) % 2
     first(slot, pairs - 1)
     second(slot, pairs - 1, w.at[1 - slot])
     last = w.at[1 - slot]
 
-    def handing(high, k):
+    def handing(to, k):
         return pltpu.make_async_remote_copy(
             last.at[own], field.at[:, pl.ds(rows, 8), :],
-            tail_send.at[high, k], tail_recv.at[block],
-            device_id=(*device_at(slab, 2 * high + core)[:4], k), device_id_type=MESH_ID,
-        )
-
-    for high in range(blocks // 2):
+            tail_send.at[to, k], tail_recv.at[block],
+            device_id=(*device_at(slab, 2 * to + core)[:4], k), device_id_type=MESH_ID,
+        )
+
+    for to in range(blocks // 2):
         for k in range(2):
 
-            @pl.when((2 * high + core != block) | (k != core))
+            @pl.when((2 * to + core != block) | (k != core))
             def _():
-                handing(high, k).start()
+                handing(to, k).start()
 
     @pl.when(same)
     def _():
@@ -369,12 +550,22 @@
 
     record(v[own], 2 * pairs - 2)
     record(last[own], 2 * pairs - 1)
-    for high in range(blocks // 2):
+    late_z[me_z, 0] = record_rows[2]
+    late_z[me_z, 1] = record_rows[3]
+    spread(3, late_z, me_z, on_z)
+    late_x[me_x] = gathered(3, late_z, me_z, on_z)
+    spread(4, late_x, me_x, on_x)
+    late_y[me_y] = gathered(4, late_x, me_x, on_x)
+    spread(5, late_y, me_y, on_y)
+    total = gathered(5, late_y, me_y, on_y)
+    put_traces(total[0], 8)
+    put_traces(total[1], 12)
+    for to in range(blocks // 2):
         for k in range(2):
 
-            @pl.when((2 * high + core != block) | (k != core))
+            @pl.when((2 * to + core != block) | (k != core))
             def _():
-                handing(high, k).wait_send()
+                handing(to, k).wait_send()
 
     for b in range(blocks):
 
@@ -387,22 +578,30 @@
             ).wait_recv()
 
 
-def wave(p_now, p_prev, velocity, wavelet, source_cell, receiver_cells):
-    vertical = p_now.shape[2]
+def per_device(
+    p_now, p_prev, velocity, density, wavelet, source_cell, receiver_cells, station_cells, observed
+):
+    planes, lateral, vertical = p_now.shape
     nrec = receiver_cells.shape[0]
     blocks = lax.axis_size("station_hi") * 2
+    nx, nz = lax.axis_size("x"), lax.axis_size("z")
+    group = station_cells.shape[0]
     f32 = jnp.float32
     padded = (24, 40, vertical)
     vmem, smem = (pl.BlockSpec(memory_space=space) for space in (pltpu.VMEM, pltpu.SMEM))
     dma = pltpu.SemaphoreType.DMA
-    return pl.pallas_call(
-        wave_kernel,
+    longest = max(nz, 2 * nx, blocks)
+    results = pl.pallas_call(
+        step_kernel,
         out_shape=(
             jax.ShapeDtypeStruct(p_now.shape, f32),
-            jax.ShapeDtypeStruct((wavelet.shape[0] * nrec // 128, 128), f32),
+            jax.ShapeDtypeStruct((wavelet.shape[0], nrec), f32),
+            jax.ShapeDtypeStruct((1, group), f32),
+            jax.ShapeDtypeStruct((planes, lateral // blocks, vertical), f32),
+            jax.ShapeDtypeStruct((3, *p_now.shape), f32),
         ),
-        in_specs=[vmem, vmem, vmem, smem, smem, vmem],
-        out_specs=(vmem, vmem),
+        in_specs=[vmem, vmem, vmem, vmem, smem, smem, vmem, vmem, vmem],
+        out_specs=(vmem,) * 5,
         scratch_shapes=[
             pltpu.VMEM((2, *padded), f32),
             pltpu.VMEM(padded, f32),
@@ -411,93 +610,33 @@
             pltpu.VMEM((8, 8, vertical), f32),
             pltpu.VMEM((8, 8, nrec), f32),
             dma((3, 3)), dma((3, 3)), dma((8,)), dma((2, 8)), dma((blocks // 2, 2)), dma((blocks,)),
+            pltpu.VMEM((blocks, 8, group), f32),
+            pltpu.VMEM((3, blocks, group), f32),
+            pltpu.VMEM((2, vertical, 128), f32),
+            pltpu.VMEM((planes * 4, 2 * vertical, blocks * group), jnp.bfloat16),
+            pltpu.VMEM((1, blocks * group), f32),
+            pltpu.VMEM((1, blocks * group), f32),
+            dma((blocks,)), dma((blocks,)),
+            pltpu.VMEM((2, planes + 2, lateral + 16, vertical), f32),
+            dma((2, 2)), dma((2, 2)),
+            pltpu.VMEM((4, 8, 128), f32),
+            *(pltpu.VMEM((n, 3, 8, 128), f32) for n in (nz, 2 * nx, blocks)),
+            *(pltpu.VMEM((n, 2, 8, 128), f32) for n in (nz, 2 * nx, blocks)),
+            dma((6, longest)), dma((6, longest)),
         ],
         compiler_params=pltpu.CompilerParams(
-            collective_id=0, has_side_effects=True, vmem_limit_bytes=32 * 2**20
+            collective_id=0, has_side_effects=True, vmem_limit_bytes=48 * 2**20
         ),
-    )(p_now, p_prev, velocity, wavelet, source_cell, receiver_cells.reshape(1, -1))
-
-
-def kernel_tile(plane_x, station_x, station_y, cell_y, cell_z):
-    delta_x = plane_x - station_x
-    delta_y = cell_y[None, :] - station_y[:, None]
-    radius_sq = (
-        delta_x[:, None] * delta_x[:, None] + delta_y * delta_y + cell_z[None, :] * cell_z[None, :]
+    )(
+        p_now, p_prev, velocity, density, wavelet, source_cell,
+        receiver_cells.reshape(1, -1), station_cells.reshape(1, -1), observed.reshape(1, -1),
     )
-    return (cell_z[None, :] / (radius_sq * jnp.sqrt(radius_sq))).astype(jnp.bfloat16)
-
-
-def cross_terms(padded, slab, lateral, vertical):
-    diff_x = (
-        padded[:, 2 : 2 + slab, 1 : 1 + lateral, 1 : 1 + vertical]
-        - padded[:, 0:slab, 1 : 1 + lateral, 1 : 1 + vertical]
-    ) * 0.5
-    diff_y = (
-        padded[:, 1 : 1 + slab, 2 : 2 + lateral, 1 : 1 + vertical]
-        - padded[:, 1 : 1 + slab, 0:lateral, 1 : 1 + vertical]
-    ) * 0.5
-    diff_z = (
-        padded[:, 1 : 1 + slab, 1 : 1 + lateral, 2 : 2 + vertical]
-        - padded[:, 1 : 1 + slab, 1 : 1 + lateral, 0:vertical]
-    ) * 0.5
-    first = diff_y[0] * diff_z[1] - diff_z[0] * diff_y[1]
-    second = diff_z[0] * diff_x[1] - diff_x[0] * diff_z[1]
-    third = diff_x[0] * diff_y[1] - diff_y[0] * diff_x[1]
-    return jnp.stack([first, second, third])
-
-
-def per_device(
-    p_now, p_prev, velocity, density, wavelet, source_cell, receiver_cells, station_cells, observed
-):
-    slab, lateral, vertical = p_now.shape
-    offset_x = lax.axis_index(MP) * slab
-    offset_y = 0
-    global_x = offset_x + jnp.arange(slab, dtype=jnp.int32)
-    global_y = offset_y + jnp.arange(lateral, dtype=jnp.int32)
-    last_field, traces = wave(p_now, p_prev, velocity, wavelet, source_cell, receiver_cells)
-    traces = lax.psum(traces, MESH).reshape(-1, receiver_cells.shape[0])
-    stacked = jnp.stack([velocity, density])
-    padded_model = extended(stacked, ((MP, 1),), 1)
-    padded_model = jnp.pad(padded_model, ((0, 0), (0, 0), (1, 1), (1, 1)))
-    cross_gradient = cross_terms(padded_model, slab, lateral, vertical)
-    station_x = (station_cells // lateral).astype(jnp.float32)
-    station_y = (station_cells % lateral).astype(jnp.float32)
-    cell_y = (jnp.arange(lateral * vertical, dtype=jnp.int32) // vertical).astype(jnp.float32)
-    cell_z = (jnp.arange(lateral * vertical, dtype=jnp.int32) % vertical).astype(jnp.float32) + 1.0
-    planes = density.astype(jnp.bfloat16).reshape(slab, lateral * vertical)
-    plane_xs = global_x.astype(jnp.float32)
-
-    def forward(totals, packed):
-        plane_x, plane = packed
-        tile = kernel_tile(plane_x, station_x, station_y, cell_y, cell_z)
-        return (totals + jnp.dot(tile, plane, preferred_element_type=jnp.float32), None)
-
-    partial_value, unused_out = lax.scan(
-        forward, jnp.zeros((station_cells.shape[0],), jnp.float32), (plane_xs, planes)
-    )
-    predicted = over_axes(partial_value, MP)
-    gravity_residual = predicted - observed
-    share_rows = lateral // lax.axis_size(STATION)
-    every_residual, every_x, every_y = turned_gather(
-        (gravity_residual, station_x, station_y), STATION, (0, 0, 0)
-    )
-    every_low = every_residual.astype(jnp.bfloat16)
-    share_index = jnp.arange(share_rows * vertical, dtype=jnp.int32)
-    share_y = (lax.axis_index(STATION) * share_rows + share_index // vertical).astype(jnp.float32)
-    share_z = (share_index % vertical).astype(jnp.float32) + 1.0
-
-    def adjoint_rows(plane_x):
-        tile = kernel_tile(plane_x, every_x, every_y, share_y, share_z)
-        return jnp.dot(every_low, tile, preferred_element_type=jnp.float32)
-
-    density_gradient = lax.map(adjoint_rows, plane_xs).reshape(slab, share_rows, vertical)
-    return (last_field, traces, gravity_residual, density_gradient, cross_gradient)
+    field, traces, residual, gradient, crossed = results
+    return field, traces, residual.reshape(-1), gradient, crossed
 
 
 def solution(mesh):
-    split = Mesh(
-        mesh.devices.reshape(*SPLIT, mesh.shape["station"] // 2, 2), MESH
-    )
+    split = Mesh(mesh.devices.reshape(*SPLIT, mesh.shape["station"] // 2, 2), MESH)
     slabs = P(MP, None, None)
     return jax.shard_map(
         per_device,

time: 299 us -> 99.2 us (0.33)
  blocking collectives: 180 us -> 0 us
  Pallas kernels: 48.8 us -> 89.8 us
  matrix products: 34.8 us -> 0 us
  other arithmetic: 15.6 us -> 0 us
  starting transfers between devices: 5.33 us -> 0 us
  local copies, waits for them, and re-layouts: 11.6 us -> 7.79 us
    psum x4 -> x0, blocking collectives: 154 us -> none  [the longest x1 112 us: per_device(): traces = lax.psum(traces, MESH).reshape(-1, receiver_cells.shape[0])]
    pallas_call x1, Pallas kernels: 48.8 us -> 89.8 us  [per_device(): pl.pallas_call(step_kernel, out_shape=(jax.ShapeDtypeStruct(p_now.shape,...]
    dot_general x16 -> x0, matrix products: 34.8 us -> none  [the longest x8 17.5 us: forward(): jnp.dot(tile, plane, preferred_element_type=jnp.float32)]
    all_gather x1 -> x0, blocking collectives: 26.3 us -> none  [turned_gather(): result = lax.all_gather(both, axis, axis=0, tiled=True)]
    dynamic_slice x16 -> x0, local copies, waits for them, and re-layouts: 9.42 us -> none  [per_device(): lax.scan(forward, jnp.zeros((station_cells.shape[0],), jnp.float32), (pla...]
    unnamed x19 -> x21, local copies, waits for them, and re-layouts: 1.46 us -> 7.79 us
    mul x26 -> x0, other arithmetic: 6.21 us -> none  [the longest x8 5.18 us: kernel_tile(): delta_x[:, None] * delta_x[:, None] + delta_y * delta_y]
    ppermute x2 -> x0, starting transfers between devices: 5.33 us -> none  [the longest x1 4.03 us: extended(): lax.ppermute(tail, axis, [(i, (i + 1) % count) for i in range(ends)])]
  transfers between devices with their start and end apart: 2 -> 0, of which waited for: 0 -> 0; matrix products, arithmetic and copies ran while one was open for 20% -> 0% of each run, Pallas kernels for 16% -> 0%
where the time goes in v2:
time: 99.2 us; the launch traced here: 98.9 us
  Pallas kernels  89.8 us (91%)
  local copies, waits for them, and re-layouts  7.79 us (8%)
  between operations  1.33 us (1%)
    pallas_call x1, Pallas kernels, per_device(): pl.pallas_call(step_kernel, out_shape=(jax.ShapeDtypeStruct(p_now.shape,...  89.8 us
    unnamed x21, local copies, waits for them, and re-layouts  7.79 us

profile of v2, /device:TPU:1, one launch (start us, length us, event | category | flops | bytes accessed | tf_op | source)
XLA Modules:
  0.0 98.9 jit_solution(16302529489111505590)
XLA Ops:
  1.3 0.0 copy-start.6
  1.3 0.0 copy-start.7
  1.3 0.0 copy-start.4
  1.3 0.0 copy-start.5
  1.3 0.6 copy-done.6
  1.9 0.0 copy-done.7
  2.0 0.0 copy-done.4
  2.0 0.0 copy-done.5
  2.0 0.0 copy-start
  2.0 0.9 copy-done
  2.9 0.0 copy-start.1
  2.9 0.9 copy-done.1
  3.9 0.0 copy-start.2
  3.9 0.9 copy-done.2
  4.8 0.0 copy-start.3
  4.8 0.9 copy-done.3
  5.8 89.8 %shard_map.128 = (f32[8,64,128]{2,1,0:T(8,128)S(1)}, f32[16,256]{1,0:T(8,128)S(1)}, f32[1,128]{1,0:T(1,128)S(1)}, f32[8,8,128]{2,1,0:T(8,128)S(1)}, f32[3,8,64,128]{3,2,1,0:T(8,128)S(1)}) custom-call(f32[8,64,128]{2,1,0:T(8,128)S(1)} %copy-done, f32[8,64,128]{2,1,0:T(8,128)S(1)} %copy-done.1, f32[8,64,128]{2,1,0:T(8,128)S(1)} %copy-done.2, ...), custom_call_target="tpu_custom_call" | custom-call | tf_op jit(solution)/shard_map/pallas_call | solution.py:594
  95.6 0.7 copy.20
  96.3 0.6 copy.21
  96.9 0.5 copy.22
  97.4 0.6 copy.23
  98.0 0.9 copy.24
Async XLA Ops:
  1.3 0.7 copy-start.6
  1.3 0.7 copy-start.7
  1.3 0.7 copy-start.4
  1.3 0.7 copy-start.5
  2.0 1.0 copy-start
  2.9 0.9 copy-start.1
  3.9 0.9 copy-start.2
  4.8 0.9 copy-start.3

commit v3 on v2

--- a/solution.py
+++ b/solution.py
@@ -59,8 +59,9 @@
     w, v, courant, mask, zmask, hits,
     init_send, init_recv, halo_send, halo_recv, tail_send, tail_recv,
     groups, stations, depth, tiles, sums, low_row, group_send, group_recv,
-    models, model_send, model_recv,
-    record_rows, early_z, early_x, early_y, late_z, late_x, late_y, ring_send, ring_recv,
+    models, model_send, model_recv, local,
+    record_rows, early_z, early_x, early_y, late_z, late_x, late_y, end_z, end_x, end_y,
+    ring_send, ring_recv, corner_out, corner_in, spreading,
 ):
     slab, block, low, core = place()
     slabs = lax.axis_size(MP)
@@ -77,16 +78,6 @@
     def window(b):
         start = jnp.clip(8 * (b - 1), 0, lateral - 24)
         return pl.multiple_of(start, 8), pl.multiple_of(ROW0 + start - 8 * b, 8)
-
-    zero = jnp.zeros((24, 24, vertical), jnp.float32)
-    for ref in (w.at[0], w.at[1], v, courant):
-        ref[:, pl.ds(8, 24), :] = zero
-
-    for n in range(2):
-        models[n, 0] = jnp.zeros(models.shape[2:], jnp.float32)
-        models[n, 9] = jnp.zeros(models.shape[2:], jnp.float32)
-        models[n, :, pl.ds(0, 8), :] = jnp.zeros((10, 8, vertical), jnp.float32)
-        models[n, :, pl.ds(8 + lateral, 8), :] = jnp.zeros((10, 8, vertical), jnp.float32)
 
     barrier = pltpu.get_barrier_semaphore()
     for other in range(2 * blocks):
@@ -138,6 +129,69 @@
     def _():
         pl.semaphore_signal(barrier, 1, device_id=far, device_id_type=MESH_ID)
 
+    start, to = window(block)
+    rows = pl.multiple_of(8 * block, 8)
+    inside = (pl.ds(1, 8), pl.ds(8, lateral))
+    loads = [
+        pltpu.make_async_copy(density, models.at[(1, *inside)], local.at[3]),
+        pltpu.make_async_copy(velocity, models.at[(0, *inside)], local.at[4]),
+    ]
+    for copy in loads:
+        copy.start()
+    inner_left = inner < 0
+
+    def local_copies(own_slab):
+        if own_slab:
+            pairs_of = [
+                (a.at[:, pl.ds(start, 24), :], p.at[pl.ds(PLANE0, 8), pl.ds(to, 24), :])
+                for a, p in ((p_now, w.at[0]), (p_prev, v), (velocity, courant))
+            ]
+        else:
+            pairs_of = [
+                (
+                    p_now.at[:, pl.ds(start, 24), :],
+                    w.at[0, pl.ds(jnp.where(inner_left, 0, 16), 8), pl.ds(to, 24), :],
+                )
+            ] + [
+                (
+                    a.at[pl.ds(jnp.where(inner_left, 4, 0), 4), pl.ds(rows, 8), :],
+                    p.at[pl.ds(jnp.where(inner_left, 4, 16), 4), pl.ds(ROW0, 8), :],
+                )
+                for a, p in ((p_prev, v), (velocity, courant))
+            ]
+        return [
+            pltpu.make_async_copy(a, b, local.at[n]) for n, (a, b) in enumerate(pairs_of)
+        ]
+
+    @pl.when(same)
+    def _():
+        for copy in local_copies(True):
+            copy.start()
+
+    @pl.when(jnp.logical_not(same))
+    def _():
+        for copy in local_copies(False):
+            copy.start()
+
+    def clear(at):
+        shape = (at[0].size, at[1].size, vertical)
+        for ref in (w.at[0], w.at[1], v, courant):
+            ref[at] = jnp.zeros(shape, jnp.float32)
+
+    pl.when(slab == 0)(lambda: clear((pl.ds(0, 8), pl.ds(8, 24))))
+    pl.when(slab == slabs - 1)(lambda: clear((pl.ds(16, 8), pl.ds(8, 24))))
+    pl.when(block == 0)(lambda: clear((pl.ds(0, 24), pl.ds(8, 8))))
+    pl.when(block == blocks - 1)(lambda: clear((pl.ds(0, 24), pl.ds(24, 8))))
+    for n in range(2):
+        for plane in (0, 9):
+
+            @pl.when(kept == (0 if plane == 0 else slabs - 1))
+            def _():
+                models[n, plane, pl.ds(8, lateral), :] = jnp.zeros((lateral, vertical), jnp.float32)
+
+        for row in (0, 8 + lateral):
+            models[n, :, pl.ds(row, 8), :] = jnp.zeros((10, 8, vertical), jnp.float32)
+
     crossing = sum(jnp.where(there(outer, db), 1, 0) for db in (-1, 0, 1))
     pl.semaphore_wait(
         barrier, 2 * blocks - 1 + crossing + nz - 1 + 2 * (nx - 1) + jnp.where(more, 1, 0)
@@ -163,49 +217,45 @@
     arrays = (p_now, p_prev, velocity)
     places = (w.at[0], v, courant)
 
-    def own_package(b, target, k):
-        start, to = window(b)
+    def own_package(n, b, target):
+        begin, landing = window(b)
+        return pltpu.make_async_remote_copy(
+            arrays[n].at[:, pl.ds(begin, 24), :],
+            places[n].at[pl.ds(PLANE0, 8), pl.ds(landing, 24), :],
+            init_send.at[3, n], init_recv.at[0, n], device_id=target, device_id_type=MESH_ID,
+        )
+
+    def halo_package(b, side, target, k, landing):
+        begin, to_row = window(b)
+        left = side < 0
+        near, far_off = jnp.where(left, 4, 0), jnp.where(left, 0, 4)
+        near_to, far_to = jnp.where(left, 4, 16), jnp.where(left, 0, 20)
+        home = pl.multiple_of(8 * b, 8)
+        block_at, block_to = pl.ds(home, 8), pl.ds(ROW0, 8)
+        parts = [
+            (p_now.at[pl.ds(near, 4), pl.ds(begin, 24), :], w.at[0, pl.ds(near_to, 4), pl.ds(to_row, 24), :]),
+            (p_now.at[pl.ds(far_off, 4), block_at, :], w.at[0, pl.ds(far_to, 4), block_to, :]),
+        ] + [
+            (a.at[pl.ds(near, 4), block_at, :], p.at[pl.ds(near_to, 4), block_to, :])
+            for a, p in ((p_prev, v), (velocity, courant))
+        ]
         return [
             pltpu.make_async_remote_copy(
-                a.at[:, pl.ds(start, 24), :],
-                p.at[pl.ds(PLANE0, 8), pl.ds(to, 24), :],
-                init_send.at[k, n], init_recv.at[0, n], device_id=target, device_id_type=MESH_ID,
-            )
-            for n, (a, p) in enumerate(zip(arrays, places))
-        ]
-
-    def halo_package(b, side, target, k, landing):
-        start, to = window(b)
-        left = side < 0
-        near_from = jnp.where(left, 4, 0)
-        near_to = jnp.where(left, 4, 16)
-        rows = pl.multiple_of(8 * b, 8)
-        copies = [
-            pltpu.make_async_remote_copy(
-                p_now.at[:, pl.ds(start, 24), :],
-                w.at[0, pl.ds(jnp.where(left, 0, 16), 8), pl.ds(to, 24), :],
-                init_send.at[k, 0], init_recv.at[landing, 0],
+                a, p, init_send.at[k, n], init_recv.at[landing, n],
                 device_id=target, device_id_type=MESH_ID,
             )
+            for n, (a, p) in enumerate(parts)
         ]
+
+    paired = block + pair
+    across = lax.rem(block - pair + blocks, blocks)
+    partner = device_at(slab, paired)
+
+    @pl.when(same)
+    def _():
+        own_package(0, paired, partner).start()
         for n in (1, 2):
-            copies.append(
-                pltpu.make_async_remote_copy(
-                    arrays[n].at[pl.ds(near_from, 4), pl.ds(rows, 8), :],
-                    places[n].at[pl.ds(near_to, 4), pl.ds(ROW0, 8), :],
-                    init_send.at[k, n], init_recv.at[landing, n],
-                    device_id=target, device_id_type=MESH_ID,
-                )
-            )
-        return copies
-
-    paired = block + pair
-    partner = device_at(slab, paired)
-
-    @pl.when(same)
-    def _():
-        for copy in own_package(paired, partner, 0):
-            copy.start()
+            own_package(n, across, device_at(slab, across)).start()
         for k, b in ((1, block), (2, paired)):
 
             @pl.when(there(outer, 0))
@@ -217,9 +267,6 @@
     def _():
         for copy in halo_package(paired, inner, partner, 0, 1):
             copy.start()
-
-    start, to = window(block)
-    rows = pl.multiple_of(8 * block, 8)
 
     def model_copy(n, outward, forth):
         e = onward if outward else -onward
@@ -233,29 +280,6 @@
             model_send.at[n, k], model_recv.at[n, k],
             device_id=far if outward else partner, device_id_type=MESH_ID,
         )
-
-    for n in range(2):
-        model_copy(n, False, True).start()
-
-        @pl.when(more)
-        def _():
-            model_copy(n, True, True).start()
-
-        models[n, pl.ds(1, 8), pl.ds(8, lateral), :] = (velocity, density)[n][...]
-
-    @pl.when(same)
-    def _():
-        for a, p in zip(arrays, places):
-            p[pl.ds(PLANE0, 8), pl.ds(to, 24), :] = a[:, pl.ds(start, 24), :]
-
-    @pl.when(jnp.logical_not(same))
-    def _():
-        left = inner < 0
-        w[0, pl.ds(jnp.where(left, 0, 16), 8), pl.ds(to, 24), :] = p_now[:, pl.ds(start, 24), :]
-        for a, p in ((p_prev, v), (velocity, courant)):
-            p[pl.ds(jnp.where(left, 4, 16), 4), pl.ds(ROW0, 8), :] = a[
-                pl.ds(jnp.where(left, 4, 0), 4), pl.ds(rows, 8), :
-            ]
 
     source_cell = source[0]
     source_z = lax.rem(source_cell, vertical)
@@ -282,38 +306,41 @@
     depth[0] = step_z
     depth[1] = step_z * step_z
     share = pl.multiple_of(8 * own_group, 8)
+    ngroups = groups.shape[0]
     sums[...] = jnp.zeros(sums.shape, jnp.float32)
-    ngroups = groups.shape[0]
+    record_rows[3] = jnp.zeros((8, 128), jnp.float32)
+    eye = lax.broadcasted_iota(jnp.int32, (128, 128), 0) == lax.broadcasted_iota(
+        jnp.int32, (128, 128), 1
+    )
+
+    def column(row):
+        picked = jnp.where(eye, jnp.broadcast_to(row, (128, 128)), 0.0).astype(jnp.bfloat16)
+        ones = jnp.ones((128, 128), jnp.bfloat16)
+        return jnp.dot(picked, ones, preferred_element_type=jnp.float32)
 
     def forward(q, unused):
         p, r = q // 4, 2 * lax.rem(q, 4)
         dx = (8 * kept + p).astype(jnp.float32) - stations[0]
-        dz, dz_sq = depth[0], depth[1]
         for u in range(2):
             dy = (share + r + u).astype(jnp.float32) - stations[1]
             flat = dx * dx + dy * dy
+            weight = column(models[1, p + 1, pl.ds(8 + share + r + u, 1), :])
             for g in range(ngroups):
-                inverse = lax.rsqrt(flat[g : g + 1, :] + dz_sq)
-                tile = (dz * inverse) * (inverse * inverse)
-                tiles[q, pl.ds(u * vertical, vertical), pl.ds(g * 128, 128)] = tile.astype(
-                    jnp.bfloat16
-                )
-        pair = jnp.concatenate(
-            [density[p, pl.ds(share + r, 1), :], density[p, pl.ds(share + r + 1, 1), :]], axis=1
-        )
-        sums[...] += jnp.dot(
-            pair.astype(jnp.bfloat16), tiles[q], preferred_element_type=jnp.float32
-        )
+                inverse = lax.rsqrt(flat[g : g + 1, :] + depth[1])
+                tile = ((depth[0] * inverse) * (inverse * inverse)).astype(jnp.bfloat16)
+                tiles[q, pl.ds(u * vertical, vertical), pl.ds(g * 128, 128)] = tile
+                part = tile.astype(jnp.float32) * weight
+                sums[g] += jnp.sum(part.reshape(vertical // 8, 8, 128), axis=0)
         return unused
 
-    def adjoint(q, unused):
-        p, r = q // 4, 2 * lax.rem(q, 4)
-        part = lax.dot_general(
-            low_row[...].astype(jnp.bfloat16), tiles[q], (((1,), (1,)), ((), ())),
-            preferred_element_type=jnp.float32,
-        )
-        gradient[p, pl.ds(r, 1), :] = part[:, :vertical]
-        gradient[p, pl.ds(r + 1, 1), :] = part[:, vertical:]
+    def adjoint(p, unused):
+        each = tiles.shape[0] // 8
+        slab_tiles = tiles[pl.ds(p * each, each)].reshape(each * 2 * vertical, ngroups * 128)
+        out = jnp.dot(slab_tiles, spreading[...], preferred_element_type=jnp.float32)
+        for r in range(2 * each):
+            unit = jnp.where(eye, out[vertical * r : vertical * (r + 1)], 0.0)
+            part = jnp.sum(unit.reshape(vertical // 8, 8, 128), axis=0)
+            gradient[p, pl.ds(r, 1), :] = jnp.sum(part, axis=0, keepdims=True)
         return unused
 
     def cross_plane(p, unused):
@@ -334,6 +361,7 @@
         crossed[2, p] = vx * qy - vy * qx
         return unused
 
+    loads[0].wait()
     for d in range(1, blocks):
         group_copy(d, True).wait_send()
         group_copy(d, False).wait_recv()
@@ -346,8 +374,9 @@
 
     @pl.when(same)
     def _():
-        for copy in own_package(paired, partner, 0):
-            copy.wait_send()
+        own_package(0, paired, partner).wait_send()
+        for n in (1, 2):
+            own_package(n, across, device_at(slab, across)).wait_send()
         for k, b in ((1, block), (2, paired)):
 
             @pl.when(there(outer, 0))
@@ -357,13 +386,17 @@
 
         for copy in halo_package(block, inner, partner, 0, 1):
             copy.wait_recv()
+        for copy in local_copies(True):
+            copy.wait()
 
     @pl.when(jnp.logical_not(same))
     def _():
         for copy in halo_package(paired, inner, partner, 0, 1):
             copy.wait_send()
-        for copy in own_package(block, partner, 0):
-            copy.wait_recv()
+        for n in range(3):
+            own_package(n, block, partner).wait_recv()
+        for copy in local_copies(False):
+            copy.wait()
 
     @pl.when(there(outer, 0))
     def _():
@@ -373,38 +406,40 @@
     scaled = TIME_RATIO * courant[:, pl.ds(8, 24), :]
     courant[:, pl.ds(8, 24), :] = scaled * scaled
 
-    def region(ds, db, near):
-        plane = PLANE0 + 8 * ds
-        count = 8
-        if near and ds:
-            plane, count = (4, 4) if ds < 0 else (16, 4)
-        return pl.ds(plane, count), pl.ds(ROW0 + 8 * db, 8)
-
-    def halo(slot, k):
+    order = (4, 5, 6, 7, 2, 3, 0, 1)
+
+    def halo(slot, k, forth):
         ds, db = SIDES[k]
-        corner = ds != 0 and db != 0
-        to = region(-ds, -db, corner)
-        if corner:
-            begin = (PLANE0, ROW0)[0] + (4 if ds > 0 else 0)
-            source_at = (pl.ds(begin, 4), pl.ds(ROW0, 8))
+        opposite = SIDES.index((-ds, -db))
+        if k >= 4:
+            begin = corner_out.at[k - 4]
+            end = corner_in.at[slot, (opposite if forth else k) - 4]
         else:
-            source_at = (pl.ds(PLANE0, 8), pl.ds(ROW0, 8))
-        opposite = SIDES.index((-ds, -db))
+            begin = w.at[slot, pl.ds(PLANE0, 8), pl.ds(ROW0, 8), :]
+            sign = -1 if forth else 1
+            end = w.at[
+                slot, pl.ds(PLANE0 + 8 * sign * ds, 8), pl.ds(ROW0 + 8 * sign * db, 8), :
+            ]
         return pltpu.make_async_remote_copy(
-            w.at[(slot, *source_at)], w.at[(slot, *to)],
-            halo_send.at[k], halo_recv.at[slot, opposite],
+            begin, end, halo_send.at[k], halo_recv.at[slot, opposite if forth else k],
             device_id=device_at(slab + ds, block + db), device_id_type=MESH_ID,
         )
 
-    def arriving(slot, k):
+    def corner_rows(k, outside):
         ds, db = SIDES[k]
-        corner = ds != 0 and db != 0
-        at = region(ds, db, corner)
-        return pltpu.make_async_remote_copy(
-            w.at[(slot, *at)], w.at[(slot, *at)],
-            halo_send.at[k], halo_recv.at[slot, k],
-            device_id=device_at(slab + ds, block + db), device_id_type=MESH_ID,
-        )
+        plane = (16 if ds > 0 else 4) if outside else (12 if ds > 0 else 8)
+        row = (24 if db > 0 else 12) if outside else (20 if db > 0 else 16)
+        return plane, row
+
+    def stage_corner(slot, k):
+        plane, row = corner_rows(k, False)
+        for n in range(4):
+            corner_out[k - 4, n // 2, pl.ds(4 * (n % 2), 4), :] = w[slot, plane + n, pl.ds(row, 4), :]
+
+    def place_corner(slot, k):
+        plane, row = corner_rows(k, True)
+        for n in range(4):
+            w[slot, plane + n, pl.ds(row, 4), :] = corner_in[slot, k - 4, n // 2, pl.ds(4 * (n % 2), 4), :]
 
     own = (pl.ds(PLANE0, 8), pl.ds(ROW0, 8))
 
@@ -457,69 +492,83 @@
         later = 1 - slot
         first(slot, m)
         second(slot, m, w.at[later])
-        for k, (ds, db) in enumerate(SIDES):
-
-            @pl.when(there(ds, db))
-            def _():
-                halo(later, k).start()
+        for k in range(4, 8):
+            stage_corner(later, k)
+        for k in order:
+
+            @pl.when(there(*SIDES[k]))
+            def _():
+                halo(later, k, True).start()
 
         record(v[own], 2 * m)
         record(w[(later, *own)], 2 * m + 1)
         background()
-        for k, (ds, db) in enumerate(SIDES):
-
-            @pl.when(there(ds, db))
-            def _():
-                halo(later, k).wait_send()
-                arriving(later, k).wait_recv()
+        for k in (0, 1, 2, 3, 4, 5, 6, 7):
+
+            @pl.when(there(*SIDES[k]))
+            def _():
+                halo(later, k, True).wait_send()
+                halo(later, k, False).wait_recv()
+                if k >= 4:
+                    place_corner(later, k)
+
+    def model_ways():
+        for n in range(2):
+            for outward in (False, True):
+                yield n, outward, (more if outward else more | True)
 
     def body(m, unused):
-        step(m, lambda: lax.fori_loop(quarter * (m + 1), quarter * (m + 2), forward, 0))
+        def background():
+            @pl.when(m == 0)
+            def _():
+                for n, outward, really in model_ways():
+
+                    @pl.when(really)
+                    def _():
+                        model_copy(n, outward, True).start()
+
+            lax.fori_loop(quarter * (m + 1), quarter * (m + 2), forward, 0)
+
+        step(m, background)
         return unused
 
     lax.fori_loop(0, 3, body, 0)
 
     def background_3():
         for g in range(ngroups):
-            early_z[me_z, 0, pl.ds(g, 1), :] = sums[:, pl.ds(g * 128, 128)]
+            early_z[me_z, 0, pl.ds(g, 1), :] = jnp.sum(sums[g], axis=0, keepdims=True)
         early_z[me_z, 1] = record_rows[0]
         early_z[me_z, 2] = record_rows[1]
         spread(0, early_z, me_z, on_z)
-        for n in range(2):
-            for outward in (False, True):
-
-                @pl.when(more | (not outward))
-                def _():
-                    model_copy(n, outward, True).wait_send()
-                    model_copy(n, outward, False).wait_recv()
+
+    def background_4():
+        loads[1].wait()
+        for n, outward, really in model_ways():
+
+            @pl.when(really)
+            def _():
+                model_copy(n, outward, True).wait_send()
+                model_copy(n, outward, False).wait_recv()
 
         lax.fori_loop(0, 8, cross_plane, 0)
 
-    def background_4():
+    def background_5():
         early_x[me_x] = gathered(0, early_z, me_z, on_z)
         spread(1, early_x, me_x, on_x)
 
-    def background_5():
+    def background_6():
+        late_z[me_z, 0] = record_rows[2]
+        late_z[me_z, 1] = record_rows[3]
+        spread(3, late_z, me_z, on_z)
         early_y[me_y] = gathered(1, early_x, me_x, on_x)
         spread(2, early_y, me_y, on_y)
 
-    def put_traces(rows_at, first_step):
-        for n in range(4):
+    def put_traces(rows_at, first_step, count):
+        for n in range(count):
             for half in range(2):
                 traces[pl.ds(first_step + n, 1), pl.ds(128 * half, 128)] = rows_at[
                     2 * n + half : 2 * n + half + 1, :
                 ]
-
-    def background_6():
-        total = gathered(2, early_y, me_y, on_y)
-        left_over = total[0, :ngroups] - stations[2]
-        stations[0] = left_over
-        residual[...] = stations[0, pl.ds(own_group, 1), :]
-        for g in range(ngroups):
-            low_row[:, pl.ds(g * 128, 128)] = left_over[g : g + 1, :]
-        put_traces(total[1], 0)
-        put_traces(total[2], 4)
-        lax.fori_loop(0, pairs_all, adjoint, 0)
 
     step(3, background_3)
     step(4, background_4)
@@ -550,16 +599,30 @@
 
     record(v[own], 2 * pairs - 2)
     record(last[own], 2 * pairs - 1)
-    late_z[me_z, 0] = record_rows[2]
-    late_z[me_z, 1] = record_rows[3]
-    spread(3, late_z, me_z, on_z)
+    end_z[me_z] = record_rows[3, pl.ds(4, 4), :]
+    spread(6, end_z, me_z, on_z)
+    total = gathered(2, early_y, me_y, on_y)
+    left_over = total[0, :ngroups] - stations[2]
+    stations[0] = left_over
+    residual[...] = stations[0, pl.ds(own_group, 1), :]
+    for g in range(ngroups):
+        spreading[pl.ds(128 * g, 128), :] = column(left_over[g : g + 1, :]).astype(jnp.bfloat16)
+    put_traces(total[1], 0, 4)
+    put_traces(total[2], 4, 4)
     late_x[me_x] = gathered(3, late_z, me_z, on_z)
     spread(4, late_x, me_x, on_x)
+    lax.fori_loop(0, 5, adjoint, 0)
+    end_x[me_x] = gathered(6, end_z, me_z, on_z)
+    spread(7, end_x, me_x, on_x)
     late_y[me_y] = gathered(4, late_x, me_x, on_x)
     spread(5, late_y, me_y, on_y)
+    lax.fori_loop(5, 8, adjoint, 0)
+    end_y[me_y] = gathered(7, end_x, me_x, on_x)
+    spread(8, end_y, me_y, on_y)
     total = gathered(5, late_y, me_y, on_y)
-    put_traces(total[0], 8)
-    put_traces(total[1], 12)
+    put_traces(total[0], 8, 4)
+    put_traces(total[1], 12, 2)
+    put_traces(gathered(8, end_y, me_y, on_y), 14, 2)
     for to in range(blocks // 2):
         for k in range(2):
 
@@ -576,6 +639,14 @@
                 tail_send.at[0, 0], tail_recv.at[b],
                 device_id=partner, device_id_type=MESH_ID,
             ).wait_recv()
+
+
+def store_kernel(*refs):
+    copies = [pltpu.make_async_copy(refs[n], refs[5 + n], refs[10].at[n]) for n in range(5)]
+    for copy in copies:
+        copy.start()
+    for copy in copies:
+        copy.wait()
 
 
 def per_device(
@@ -589,6 +660,7 @@
     f32 = jnp.float32
     padded = (24, 40, vertical)
     vmem, smem = (pl.BlockSpec(memory_space=space) for space in (pltpu.VMEM, pltpu.SMEM))
+    hbm = pl.BlockSpec(memory_space=pltpu.HBM)
     dma = pltpu.SemaphoreType.DMA
     longest = max(nz, 2 * nx, blocks)
     results = pl.pallas_call(
@@ -600,7 +672,7 @@
             jax.ShapeDtypeStruct((planes, lateral // blocks, vertical), f32),
             jax.ShapeDtypeStruct((3, *p_now.shape), f32),
         ),
-        in_specs=[vmem, vmem, vmem, vmem, smem, smem, vmem, vmem, vmem],
+        in_specs=[hbm, hbm, hbm, hbm, smem, smem, vmem, vmem, vmem],
         out_specs=(vmem,) * 5,
         scratch_shapes=[
             pltpu.VMEM((2, *padded), f32),
@@ -609,29 +681,40 @@
             pltpu.VMEM(padded, f32),
             pltpu.VMEM((8, 8, vertical), f32),
             pltpu.VMEM((8, 8, nrec), f32),
-            dma((3, 3)), dma((3, 3)), dma((8,)), dma((2, 8)), dma((blocks // 2, 2)), dma((blocks,)),
+            dma((4, 4)), dma((3, 4)), dma((8,)), dma((2, 8)), dma((blocks // 2, 2)), dma((blocks,)),
             pltpu.VMEM((blocks, 8, group), f32),
             pltpu.VMEM((3, blocks, group), f32),
             pltpu.VMEM((2, vertical, 128), f32),
             pltpu.VMEM((planes * 4, 2 * vertical, blocks * group), jnp.bfloat16),
-            pltpu.VMEM((1, blocks * group), f32),
+            pltpu.VMEM((blocks, 8, group), f32),
             pltpu.VMEM((1, blocks * group), f32),
             dma((blocks,)), dma((blocks,)),
             pltpu.VMEM((2, planes + 2, lateral + 16, vertical), f32),
-            dma((2, 2)), dma((2, 2)),
+            dma((2, 2)), dma((2, 2)), dma((5,)),
             pltpu.VMEM((4, 8, 128), f32),
             *(pltpu.VMEM((n, 3, 8, 128), f32) for n in (nz, 2 * nx, blocks)),
             *(pltpu.VMEM((n, 2, 8, 128), f32) for n in (nz, 2 * nx, blocks)),
-            dma((6, longest)), dma((6, longest)),
+            *(pltpu.VMEM((n, 4, 128), f32) for n in (nz, 2 * nx, blocks)),
+            dma((9, longest)), dma((9, longest)),
+            pltpu.VMEM((4, 2, 8, vertical), f32),
+            pltpu.VMEM((2, 4, 2, 8, vertical), f32),
+            pltpu.VMEM((blocks * group, 128), jnp.bfloat16),
         ],
         compiler_params=pltpu.CompilerParams(
             collective_id=0, has_side_effects=True, vmem_limit_bytes=48 * 2**20
         ),
     )(
-        p_now, p_prev, velocity, density, wavelet, source_cell,
+        *(pltpu.with_memory_space_constraint(a, pltpu.HBM) for a in (p_now, p_prev, velocity, density)), wavelet, source_cell,
         receiver_cells.reshape(1, -1), station_cells.reshape(1, -1), observed.reshape(1, -1),
     )
-    field, traces, residual, gradient, crossed = results
+    field, traces, residual, gradient, crossed = pl.pallas_call(
+        store_kernel,
+        out_shape=tuple(jax.ShapeDtypeStruct(r.shape, r.dtype) for r in results),
+        in_specs=[vmem] * 5,
+        out_specs=(hbm,) * 5,
+        scratch_shapes=[dma((5,))],
+        compiler_params=pltpu.CompilerParams(vmem_limit_bytes=2 * 2**20),
+    )(*results)
     return field, traces, residual.reshape(-1), gradient, crossed
 
 

time: 99.2 us -> 82.7 us (0.83)
  Pallas kernels: 89.8 us -> 80.5 us
  local copies, waits for them, and re-layouts: 7.79 us -> 0.68 us
    pallas_call x1, Pallas kernels: 89.8 us -> 79.5 us  [per_device(): pl.pallas_call(step_kernel, out_shape=(jax.ShapeDtypeStruct(p_now.shape,...]
    unnamed x21 -> x8, local copies, waits for them, and re-layouts: 7.79 us -> 0.68 us
    pallas_call x0 -> x1, Pallas kernels: none -> 1.03 us  [per_device(): pl.pallas_call(store_kernel, out_shape=tuple((jax.ShapeDtypeStruct(r.shap...]
where the time goes in v3:
time: 82.7 us; the launch traced here: 82.5 us
  Pallas kernels  80.5 us (97%)
  between operations  1.32 us (2%)
    pallas_call x1, Pallas kernels, per_device(): pl.pallas_call(step_kernel, out_shape=(jax.ShapeDtypeStruct(p_now.shape,...  79.5 us

profile of v3, /device:TPU:1, one launch (start us, length us, event | category | flops | bytes accessed | tf_op | source)
XLA Modules:
  0.0 82.5 jit_solution(14679481188878166626)
XLA Ops:
  1.3 0.0 copy-start.2
  1.3 0.0 copy-start.3
  1.3 0.0 copy-start
  1.3 0.0 copy-start.1
  1.3 0.6 copy-done.2
  1.9 0.0 copy-done.3
  2.0 0.0 copy-done
  2.0 0.0 copy-done.1
  2.0 79.5 %shard_map.128 = (f32[8,64,128]{2,1,0:T(8,128)S(1)}, f32[16,256]{1,0:T(8,128)S(1)}, f32[1,128]{1,0:T(1,128)S(1)}, f32[8,8,128]{2,1,0:T(8,128)S(1)}, f32[3,8,64,128]{3,2,1,0:T(8,128)S(1)}) custom-call(f32[8,64,128]{2,1,0:T(8,128)} %p_now.1, f32[8,64,128]{2,1,0:T(8,128)} %p_prev.1, f32[8,64,128]{2,1,0:T(8,128)} %velocity.1, f32[8,64,128]{2,1,0:T(8,128)} %density.1, ...), custom_call_target="tpu_custom_call" | custom-call | tf_op jit(solution)/shard_map/pallas_call | solution.py:666
  81.5 1.0 %shard_map.129 = (f32[8,64,128]{2,1,0:T(8,128)}, f32[16,256]{1,0:T(8,128)}, f32[1,128]{1,0:T(1,128)}, f32[8,8,128]{2,1,0:T(8,128)}, f32[3,8,64,128]{3,2,1,0:T(8,128)}) custom-call(f32[8,64,128]{2,1,0:T(8,128)S(1)} %get-tuple-element.15.refs_0_, f32[16,256]{1,0:T(8,128)S(1)} %get-tuple-element.16.refs_1_, f32[1,128]{1,0:T(1,128)S(1)} %get-tuple-element.17.refs_2_, ...), custom_call_target="tpu_custom_call" | custom-call | tf_op jit(solution)/shard_map/pallas_call | solution.py:710
Async XLA Ops:
  1.3 0.7 copy-start.2
  1.3 0.7 copy-start.3
  1.3 0.7 copy-start
  1.3 0.7 copy-start.1

commit v4 on v3

--- a/solution.py
+++ b/solution.py
@@ -54,8 +54,9 @@
 
 
 def step_kernel(
-    p_now, p_prev, velocity, density, wavelet, source, receivers, cells, observed,
+    p_now, p_prev, velocity, density, wavelet, source, receivers_in, cells_in, observed_in,
     field, traces, residual, gradient, crossed,
+    receivers, cells, observed, small,
     w, v, courant, mask, zmask, hits,
     init_send, init_recv, halo_send, halo_recv, tail_send, tail_recv,
     groups, stations, depth, tiles, sums, low_row, group_send, group_recv,
@@ -128,6 +129,17 @@
     @pl.when(more)
     def _():
         pl.semaphore_signal(barrier, 1, device_id=far, device_id_type=MESH_ID)
+
+    smalls = [
+        pltpu.make_async_copy(a, b, small.at[n])
+        for n, (a, b) in enumerate(
+            (
+                (cells_in, cells), (observed_in, observed), (receivers_in, receivers),
+            )
+        )
+    ]
+    for copy in smalls:
+        copy.start()
 
     start, to = window(block)
     rows = pl.multiple_of(8 * block, 8)
@@ -198,6 +210,8 @@
     )
 
     own_group = 2 * high + core
+    smalls[0].wait()
+    smalls[1].wait()
     sizes = (lateral.bit_length() - 1, lateral - 1)
     groups[own_group, pl.ds(0, 1), :] = (cells[...] >> sizes[0]).astype(jnp.float32)
     groups[own_group, pl.ds(1, 1), :] = (cells[...] & sizes[1]).astype(jnp.float32)
@@ -281,6 +295,8 @@
             device_id=far if outward else partner, device_id_type=MESH_ID,
         )
 
+    for copy in smalls[2:]:
+        copy.wait()
     source_cell = source[0]
     source_z = lax.rem(source_cell, vertical)
     source_xy = source_cell // vertical
@@ -369,8 +385,8 @@
         for n in range(3):
             stations[n, pl.ds(g, 1), :] = groups[g, pl.ds(n, 1), :]
     pairs_all = tiles.shape[0]
-    quarter = pairs_all // 4
-    lax.fori_loop(0, quarter, forward, 0)
+    share_of = pairs_all * 3 // 16
+    lax.fori_loop(0, share_of, forward, 0)
 
     @pl.when(same)
     def _():
@@ -519,7 +535,7 @@
 
     def body(m, unused):
         def background():
-            @pl.when(m == 0)
+            @pl.when(m == 1)
             def _():
                 for n, outward, really in model_ways():
 
@@ -527,21 +543,22 @@
                     def _():
                         model_copy(n, outward, True).start()
 
-            lax.fori_loop(quarter * (m + 1), quarter * (m + 2), forward, 0)
+            lax.fori_loop(share_of * (m + 1), share_of * (m + 2), forward, 0)
 
         step(m, background)
         return unused
 
-    lax.fori_loop(0, 3, body, 0)
-
-    def background_3():
+    lax.fori_loop(0, 4, body, 0)
+
+    def background_4():
+        lax.fori_loop(share_of * 5, pairs_all, forward, 0)
         for g in range(ngroups):
             early_z[me_z, 0, pl.ds(g, 1), :] = jnp.sum(sums[g], axis=0, keepdims=True)
         early_z[me_z, 1] = record_rows[0]
         early_z[me_z, 2] = record_rows[1]
         spread(0, early_z, me_z, on_z)
 
-    def background_4():
+    def background_5():
         loads[1].wait()
         for n, outward, really in model_ways():
 
@@ -551,17 +568,13 @@
                 model_copy(n, outward, False).wait_recv()
 
         lax.fori_loop(0, 8, cross_plane, 0)
-
-    def background_5():
-        early_x[me_x] = gathered(0, early_z, me_z, on_z)
-        spread(1, early_x, me_x, on_x)
 
     def background_6():
         late_z[me_z, 0] = record_rows[2]
         late_z[me_z, 1] = record_rows[3]
+        early_x[me_x] = gathered(0, early_z, me_z, on_z)
+        spread(1, early_x, me_x, on_x)
         spread(3, late_z, me_z, on_z)
-        early_y[me_y] = gathered(1, early_x, me_x, on_x)
-        spread(2, early_y, me_y, on_y)
 
     def put_traces(rows_at, first_step, count):
         for n in range(count):
@@ -570,7 +583,6 @@
                     2 * n + half : 2 * n + half + 1, :
                 ]
 
-    step(3, background_3)
     step(4, background_4)
     step(5, background_5)
     step(6, background_6)
@@ -601,6 +613,10 @@
     record(last[own], 2 * pairs - 1)
     end_z[me_z] = record_rows[3, pl.ds(4, 4), :]
     spread(6, end_z, me_z, on_z)
+    early_y[me_y] = gathered(1, early_x, me_x, on_x)
+    spread(2, early_y, me_y, on_y)
+    late_x[me_x] = gathered(3, late_z, me_z, on_z)
+    spread(4, late_x, me_x, on_x)
     total = gathered(2, early_y, me_y, on_y)
     left_over = total[0, :ngroups] - stations[2]
     stations[0] = left_over
@@ -609,16 +625,14 @@
         spreading[pl.ds(128 * g, 128), :] = column(left_over[g : g + 1, :]).astype(jnp.bfloat16)
     put_traces(total[1], 0, 4)
     put_traces(total[2], 4, 4)
-    late_x[me_x] = gathered(3, late_z, me_z, on_z)
-    spread(4, late_x, me_x, on_x)
-    lax.fori_loop(0, 5, adjoint, 0)
     end_x[me_x] = gathered(6, end_z, me_z, on_z)
     spread(7, end_x, me_x, on_x)
     late_y[me_y] = gathered(4, late_x, me_x, on_x)
     spread(5, late_y, me_y, on_y)
-    lax.fori_loop(5, 8, adjoint, 0)
+    lax.fori_loop(0, 4, adjoint, 0)
     end_y[me_y] = gathered(7, end_x, me_x, on_x)
     spread(8, end_y, me_y, on_y)
+    lax.fori_loop(4, 8, adjoint, 0)
     total = gathered(5, late_y, me_y, on_y)
     put_traces(total[0], 8, 4)
     put_traces(total[1], 12, 2)
@@ -647,6 +661,10 @@
         copy.start()
     for copy in copies:
         copy.wait()
+
+
+def in_hbm(array):
+    return pltpu.with_memory_space_constraint(array, pltpu.HBM)
 
 
 def per_device(
@@ -672,9 +690,11 @@
             jax.ShapeDtypeStruct((planes, lateral // blocks, vertical), f32),
             jax.ShapeDtypeStruct((3, *p_now.shape), f32),
         ),
-        in_specs=[hbm, hbm, hbm, hbm, smem, smem, vmem, vmem, vmem],
+        in_specs=[hbm] * 4 + [smem] * 2 + [hbm] * 3,
         out_specs=(vmem,) * 5,
         scratch_shapes=[
+            pltpu.VMEM((1, nrec), jnp.int32), pltpu.VMEM((1, group), jnp.int32),
+            pltpu.VMEM((1, group), f32), dma((3,)),
             pltpu.VMEM((2, *padded), f32),
             pltpu.VMEM(padded, f32),
             pltpu.VMEM(padded, f32),
@@ -704,8 +724,8 @@
             collective_id=0, has_side_effects=True, vmem_limit_bytes=48 * 2**20
         ),
     )(
-        *(pltpu.with_memory_space_constraint(a, pltpu.HBM) for a in (p_now, p_prev, velocity, density)), wavelet, source_cell,
-        receiver_cells.reshape(1, -1), station_cells.reshape(1, -1), observed.reshape(1, -1),
+        *map(in_hbm, (p_now, p_prev, velocity, density)), wavelet, source_cell,
+        *(in_hbm(a.reshape(1, -1)) for a in (receiver_cells, station_cells, observed)),
     )
     field, traces, residual, gradient, crossed = pl.pallas_call(
         store_kernel,

time: 82.7 us -> 87.4 us (1.057)
  Pallas kernels: 80.5 us -> 85.3 us
    pallas_call x1, Pallas kernels: 79.5 us -> 84.3 us  [per_device(): pl.pallas_call(step_kernel, out_shape=(jax.ShapeDtypeStruct(p_now.shape,...]
where the time goes in v4:
time: 87.4 us; the launch traced here: 87.3 us
  Pallas kernels  85.3 us (98%)
  between operations  1.3 us (1%)
    pallas_call x1, Pallas kernels, per_device(): pl.pallas_call(step_kernel, out_shape=(jax.ShapeDtypeStruct(p_now.shape,...  84.3 us

profile of v4, /device:TPU:1, one launch (start us, length us, event | category | flops | bytes accessed | tf_op | source)
XLA Modules:
  0.0 87.3 jit_solution(16008206995254309626)
XLA Ops:
  1.3 0.0 copy-start
  1.3 0.6 copy-done
  1.9 84.3 %shard_map.128 = (f32[8,64,128]{2,1,0:T(8,128)S(1)}, f32[16,256]{1,0:T(8,128)S(1)}, f32[1,128]{1,0:T(1,128)S(1)}, f32[8,8,128]{2,1,0:T(8,128)S(1)}, f32[3,8,64,128]{3,2,1,0:T(8,128)S(1)}) custom-call(f32[8,64,128]{2,1,0:T(8,128)} %p_now.1, f32[8,64,128]{2,1,0:T(8,128)} %p_prev.1, f32[8,64,128]{2,1,0:T(8,128)} %velocity.1, f32[8,64,128]{2,1,0:T(8,128)} %density.1, ...), custom_call_target="tpu_custom_call" | custom-call | tf_op jit(solution)/shard_map/pallas_call | solution.py:684
  86.2 1.0 %shard_map.129 = (f32[8,64,128]{2,1,0:T(8,128)}, f32[16,256]{1,0:T(8,128)}, f32[1,128]{1,0:T(1,128)}, f32[8,8,128]{2,1,0:T(8,128)}, f32[3,8,64,128]{3,2,1,0:T(8,128)}) custom-call(f32[8,64,128]{2,1,0:T(8,128)S(1)} %get-tuple-element.15.refs_0_, f32[16,256]{1,0:T(8,128)S(1)} %get-tuple-element.16.refs_1_, f32[1,128]{1,0:T(1,128)S(1)} %get-tuple-element.17.refs_2_, ...), custom_call_target="tpu_custom_call" | custom-call | tf_op jit(solution)/shard_map/pallas_call | solution.py:730
Async XLA Ops:
  1.3 0.7 copy-start

commit v5 on v4

--- a/solution.py
+++ b/solution.py
@@ -61,7 +61,7 @@
     init_send, init_recv, halo_send, halo_recv, tail_send, tail_recv,
     groups, stations, depth, tiles, sums, low_row, group_send, group_recv,
     models, model_send, model_recv, local,
-    record_rows, early_z, early_x, early_y, late_z, late_x, late_y, end_z, end_x, end_y,
+    record_rows, early_z, early_x, early_y, late_z, late_x, late_y, end_z,
     ring_send, ring_recv, corner_out, corner_in, spreading,
 ):
     slab, block, low, core = place()
@@ -385,7 +385,7 @@
         for n in range(3):
             stations[n, pl.ds(g, 1), :] = groups[g, pl.ds(n, 1), :]
     pairs_all = tiles.shape[0]
-    share_of = pairs_all * 3 // 16
+    share_of = pairs_all // 4
     lax.fori_loop(0, share_of, forward, 0)
 
     @pl.when(same)
@@ -466,12 +466,32 @@
             row = n * (nrec // 128) + half
             record_rows[row // 8, pl.ds(lax.rem(row, 8), 1), :] = jnp.sum(part, axis=0, keepdims=True)
 
-    def first(slot, m):
+    def settle(slot, sides):
+        for k in sides:
+
+            @pl.when(there(*SIDES[k]))
+            def _():
+                halo(slot, k, False).wait_recv()
+                if k >= 4:
+                    place_corner(slot, k)
+
+    def sent(slot):
+        for k in order:
+
+            @pl.when(there(*SIDES[k]))
+            def _():
+                halo(slot, k, True).wait_send()
+
+    def first(slot, m, arriving):
         pulse = wavelet[2 * m]
         here = w.at[slot]
+        if arriving:
+            settle(slot, (0, 1, 4, 5, 6, 7))
         for p0 in (4, 16):
             new = advance(here, v, courant, mask, pulse, zmask, p0, 4, ROW0)
             v[pl.ds(p0, 4), pl.ds(ROW0, 8), :] = new
+        if arriving:
+            settle(slot, (2, 3))
         for p0 in range(8, 16, 2):
             for r0 in (12, 20):
                 new = advance(here, v, courant, mask, pulse, zmask, p0, 2, r0)
@@ -503,11 +523,13 @@
             ring(k, buffer, me, buffer.shape[0], address, False, d).wait_recv()
         return total_of(buffer)
 
-    def step(m, background):
+    def step(m, background, arriving=True):
         slot = lax.rem(m, 2)
         later = 1 - slot
-        first(slot, m)
+        first(slot, m, arriving)
         second(slot, m, w.at[later])
+        if arriving:
+            sent(slot)
         for k in range(4, 8):
             stage_corner(later, k)
         for k in order:
@@ -519,46 +541,36 @@
         record(v[own], 2 * m)
         record(w[(later, *own)], 2 * m + 1)
         background()
-        for k in (0, 1, 2, 3, 4, 5, 6, 7):
-
-            @pl.when(there(*SIDES[k]))
-            def _():
-                halo(later, k, True).wait_send()
-                halo(later, k, False).wait_recv()
-                if k >= 4:
-                    place_corner(later, k)
 
     def model_ways():
         for n in range(2):
             for outward in (False, True):
                 yield n, outward, (more if outward else more | True)
 
+    def gravity_share(m):
+        lax.fori_loop(share_of * (m + 1), share_of * (m + 2), forward, 0)
+
+    def background_0():
+        for n, outward, really in model_ways():
+
+            @pl.when(really)
+            def _():
+                model_copy(n, outward, True).start()
+
+        gravity_share(0)
+
     def body(m, unused):
-        def background():
-            @pl.when(m == 1)
-            def _():
-                for n, outward, really in model_ways():
-
-                    @pl.when(really)
-                    def _():
-                        model_copy(n, outward, True).start()
-
-            lax.fori_loop(share_of * (m + 1), share_of * (m + 2), forward, 0)
-
-        step(m, background)
+        step(m, lambda: gravity_share(m))
         return unused
 
-    lax.fori_loop(0, 4, body, 0)
-
-    def background_4():
-        lax.fori_loop(share_of * 5, pairs_all, forward, 0)
+    def background_3():
         for g in range(ngroups):
             early_z[me_z, 0, pl.ds(g, 1), :] = jnp.sum(sums[g], axis=0, keepdims=True)
         early_z[me_z, 1] = record_rows[0]
         early_z[me_z, 2] = record_rows[1]
         spread(0, early_z, me_z, on_z)
 
-    def background_5():
+    def background_4():
         loads[1].wait()
         for n, outward, really in model_ways():
 
@@ -569,11 +581,15 @@
 
         lax.fori_loop(0, 8, cross_plane, 0)
 
+    def background_5():
+        early_x[me_x] = gathered(0, early_z, me_z, on_z)
+        spread(1, early_x, me_x, on_x)
+
     def background_6():
+        early_y[me_y] = gathered(1, early_x, me_x, on_x)
+        spread(2, early_y, me_y, on_y)
         late_z[me_z, 0] = record_rows[2]
         late_z[me_z, 1] = record_rows[3]
-        early_x[me_x] = gathered(0, early_z, me_z, on_z)
-        spread(1, early_x, me_x, on_x)
         spread(3, late_z, me_z, on_z)
 
     def put_traces(rows_at, first_step, count):
@@ -583,12 +599,16 @@
                     2 * n + half : 2 * n + half + 1, :
                 ]
 
+    step(0, background_0, False)
+    lax.fori_loop(1, 3, body, 0)
+    step(3, background_3)
     step(4, background_4)
     step(5, background_5)
     step(6, background_6)
     slot = (pairs - 1) % 2
-    first(slot, pairs - 1)
+    first(slot, pairs - 1, True)
     second(slot, pairs - 1, w.at[1 - slot])
+    sent(slot)
     last = w.at[1 - slot]
 
     def handing(to, k):
@@ -613,10 +633,6 @@
     record(last[own], 2 * pairs - 1)
     end_z[me_z] = record_rows[3, pl.ds(4, 4), :]
     spread(6, end_z, me_z, on_z)
-    early_y[me_y] = gathered(1, early_x, me_x, on_x)
-    spread(2, early_y, me_y, on_y)
-    late_x[me_x] = gathered(3, late_z, me_z, on_z)
-    spread(4, late_x, me_x, on_x)
     total = gathered(2, early_y, me_y, on_y)
     left_over = total[0, :ngroups] - stations[2]
     stations[0] = left_over
@@ -625,18 +641,17 @@
         spreading[pl.ds(128 * g, 128), :] = column(left_over[g : g + 1, :]).astype(jnp.bfloat16)
     put_traces(total[1], 0, 4)
     put_traces(total[2], 4, 4)
-    end_x[me_x] = gathered(6, end_z, me_z, on_z)
-    spread(7, end_x, me_x, on_x)
+    lax.fori_loop(0, 4, adjoint, 0)
+    late_x[me_x] = gathered(3, late_z, me_z, on_z)
+    late_x[me_x, 1, pl.ds(4, 4), :] = gathered(6, end_z, me_z, on_z)
+    spread(4, late_x, me_x, on_x)
+    lax.fori_loop(4, 7, adjoint, 0)
     late_y[me_y] = gathered(4, late_x, me_x, on_x)
     spread(5, late_y, me_y, on_y)
-    lax.fori_loop(0, 4, adjoint, 0)
-    end_y[me_y] = gathered(7, end_x, me_x, on_x)
-    spread(8, end_y, me_y, on_y)
-    lax.fori_loop(4, 8, adjoint, 0)
+    lax.fori_loop(7, 8, adjoint, 0)
     total = gathered(5, late_y, me_y, on_y)
     put_traces(total[0], 8, 4)
-    put_traces(total[1], 12, 2)
-    put_traces(gathered(8, end_y, me_y, on_y), 14, 2)
+    put_traces(total[1], 12, 4)
     for to in range(blocks // 2):
         for k in range(2):
 
@@ -714,8 +729,8 @@
             pltpu.VMEM((4, 8, 128), f32),
             *(pltpu.VMEM((n, 3, 8, 128), f32) for n in (nz, 2 * nx, blocks)),
             *(pltpu.VMEM((n, 2, 8, 128), f32) for n in (nz, 2 * nx, blocks)),
-            *(pltpu.VMEM((n, 4, 128), f32) for n in (nz, 2 * nx, blocks)),
-            dma((9, longest)), dma((9, longest)),
+            pltpu.VMEM((nz, 4, 128), f32),
+            dma((7, longest)), dma((7, longest)),
             pltpu.VMEM((4, 2, 8, vertical), f32),
             pltpu.VMEM((2, 4, 2, 8, vertical), f32),
             pltpu.VMEM((blocks * group, 128), jnp.bfloat16),

time: 87.4 us -> 82.3 us (0.942)
  Pallas kernels: 85.3 us -> 80.2 us
    pallas_call x1, Pallas kernels: 84.3 us -> 79.2 us  [per_device(): pl.pallas_call(step_kernel, out_shape=(jax.ShapeDtypeStruct(p_now.shape,...]
where the time goes in v5:
time: 82.3 us; the launch traced here: 82.1 us
  Pallas kernels  80.2 us (97%)
  between operations  1.3 us (2%)
    pallas_call x1, Pallas kernels, per_device(): pl.pallas_call(step_kernel, out_shape=(jax.ShapeDtypeStruct(p_now.shape,...  79.2 us

profile of v5, /device:TPU:1, one launch (start us, length us, event | category | flops | bytes accessed | tf_op | source)
XLA Modules:
  0.0 82.1 jit_solution(11882123424512277204)
XLA Ops:
  1.3 0.0 copy-start
  1.3 0.6 copy-done
  1.9 79.2 %shard_map.128 = (f32[8,64,128]{2,1,0:T(8,128)S(1)}, f32[16,256]{1,0:T(8,128)S(1)}, f32[1,128]{1,0:T(1,128)S(1)}, f32[8,8,128]{2,1,0:T(8,128)S(1)}, f32[3,8,64,128]{3,2,1,0:T(8,128)S(1)}) custom-call(f32[8,64,128]{2,1,0:T(8,128)} %p_now.1, f32[8,64,128]{2,1,0:T(8,128)} %p_prev.1, f32[8,64,128]{2,1,0:T(8,128)} %velocity.1, f32[8,64,128]{2,1,0:T(8,128)} %density.1, ...), custom_call_target="tpu_custom_call" | custom-call | tf_op jit(solution)/shard_map/pallas_call | solution.py:699
  81.1 1.0 %shard_map.129 = (f32[8,64,128]{2,1,0:T(8,128)}, f32[16,256]{1,0:T(8,128)}, f32[1,128]{1,0:T(1,128)}, f32[8,8,128]{2,1,0:T(8,128)}, f32[3,8,64,128]{3,2,1,0:T(8,128)}) custom-call(f32[8,64,128]{2,1,0:T(8,128)S(1)} %get-tuple-element.15.refs_0_, f32[16,256]{1,0:T(8,128)S(1)} %get-tuple-element.16.refs_1_, f32[1,128]{1,0:T(1,128)S(1)} %get-tuple-element.17.refs_2_, ...), custom_call_target="tpu_custom_call" | custom-call | tf_op jit(solution)/shard_map/pallas_call | solution.py:745
Async XLA Ops:
  1.3 0.7 copy-start

commit v6 on v5

--- a/solution.py
+++ b/solution.py
@@ -385,8 +385,8 @@
         for n in range(3):
             stations[n, pl.ds(g, 1), :] = groups[g, pl.ds(n, 1), :]
     pairs_all = tiles.shape[0]
-    share_of = pairs_all // 4
-    lax.fori_loop(0, share_of, forward, 0)
+    at_first, share_of = pairs_all // 8, pairs_all * 3 // 16
+    lax.fori_loop(0, at_first, forward, 0)
 
     @pl.when(same)
     def _():
@@ -548,7 +548,7 @@
                 yield n, outward, (more if outward else more | True)
 
     def gravity_share(m):
-        lax.fori_loop(share_of * (m + 1), share_of * (m + 2), forward, 0)
+        lax.fori_loop(at_first + share_of * m, at_first + share_of * (m + 1), forward, 0)
 
     def background_0():
         for n, outward, really in model_ways():
@@ -563,14 +563,15 @@
         step(m, lambda: gravity_share(m))
         return unused
 
-    def background_3():
+    def background_4():
+        lax.fori_loop(at_first + share_of * 4, pairs_all, forward, 0)
         for g in range(ngroups):
             early_z[me_z, 0, pl.ds(g, 1), :] = jnp.sum(sums[g], axis=0, keepdims=True)
         early_z[me_z, 1] = record_rows[0]
         early_z[me_z, 2] = record_rows[1]
         spread(0, early_z, me_z, on_z)
 
-    def background_4():
+    def background_5():
         loads[1].wait()
         for n, outward, really in model_ways():
 
@@ -581,13 +582,9 @@
 
         lax.fori_loop(0, 8, cross_plane, 0)
 
-    def background_5():
+    def background_6():
         early_x[me_x] = gathered(0, early_z, me_z, on_z)
         spread(1, early_x, me_x, on_x)
-
-    def background_6():
-        early_y[me_y] = gathered(1, early_x, me_x, on_x)
-        spread(2, early_y, me_y, on_y)
         late_z[me_z, 0] = record_rows[2]
         late_z[me_z, 1] = record_rows[3]
         spread(3, late_z, me_z, on_z)
@@ -600,8 +597,7 @@
                 ]
 
     step(0, background_0, False)
-    lax.fori_loop(1, 3, body, 0)
-    step(3, background_3)
+    lax.fori_loop(1, 4, body, 0)
     step(4, background_4)
     step(5, background_5)
     step(6, background_6)
@@ -618,21 +614,23 @@
             device_id=(*device_at(slab, 2 * to + core)[:4], k), device_id_type=MESH_ID,
         )
 
-    for to in range(blocks // 2):
-        for k in range(2):
-
-            @pl.when((2 * to + core != block) | (k != core))
-            def _():
-                handing(to, k).start()
-
-    @pl.when(same)
-    def _():
-        field[:, pl.ds(rows, 8), :] = last[own]
-
     record(v[own], 2 * pairs - 2)
     record(last[own], 2 * pairs - 1)
     end_z[me_z] = record_rows[3, pl.ds(4, 4), :]
     spread(6, end_z, me_z, on_z)
+    early_y[me_y] = gathered(1, early_x, me_x, on_x)
+    spread(2, early_y, me_y, on_y)
+    for to in range(blocks // 2):
+        for k in range(2):
+
+            @pl.when((2 * to + core != block) | (k != core))
+            def _():
+                handing(to, k).start()
+
+    @pl.when(same)
+    def _():
+        field[:, pl.ds(rows, 8), :] = last[own]
+
     total = gathered(2, early_y, me_y, on_y)
     left_over = total[0, :ngroups] - stations[2]
     stations[0] = left_over
@@ -641,14 +639,13 @@
         spreading[pl.ds(128 * g, 128), :] = column(left_over[g : g + 1, :]).astype(jnp.bfloat16)
     put_traces(total[1], 0, 4)
     put_traces(total[2], 4, 4)
-    lax.fori_loop(0, 4, adjoint, 0)
     late_x[me_x] = gathered(3, late_z, me_z, on_z)
     late_x[me_x, 1, pl.ds(4, 4), :] = gathered(6, end_z, me_z, on_z)
     spread(4, late_x, me_x, on_x)
-    lax.fori_loop(4, 7, adjoint, 0)
+    lax.fori_loop(0, 4, adjoint, 0)
     late_y[me_y] = gathered(4, late_x, me_x, on_x)
     spread(5, late_y, me_y, on_y)
-    lax.fori_loop(7, 8, adjoint, 0)
+    lax.fori_loop(4, 8, adjoint, 0)
     total = gathered(5, late_y, me_y, on_y)
     put_traces(total[0], 8, 4)
     put_traces(total[1], 12, 4)

time: 82.3 us -> 83.4 us (1.013)
  Pallas kernels: 80.2 us -> 81.3 us
    pallas_call x1, Pallas kernels: 79.2 us -> 80.3 us  [per_device(): pl.pallas_call(step_kernel, out_shape=(jax.ShapeDtypeStruct(p_now.shape,...]
where the time goes in v6:
time: 83.4 us; the launch traced here: 83.3 us
  Pallas kernels  81.3 us (97%)
  between operations  1.3 us (2%)
    pallas_call x1, Pallas kernels, per_device(): pl.pallas_call(step_kernel, out_shape=(jax.ShapeDtypeStruct(p_now.shape,...  80.3 us

profile of v6, /device:TPU:1, one launch (start us, length us, event | category | flops | bytes accessed | tf_op | source)
XLA Modules:
  0.0 83.3 jit_solution(3888315864870982231)
XLA Ops:
  1.3 0.0 copy-start
  1.3 0.6 copy-done
  1.9 80.3 %shard_map.128 = (f32[8,64,128]{2,1,0:T(8,128)S(1)}, f32[16,256]{1,0:T(8,128)S(1)}, f32[1,128]{1,0:T(1,128)S(1)}, f32[8,8,128]{2,1,0:T(8,128)S(1)}, f32[3,8,64,128]{3,2,1,0:T(8,128)S(1)}) custom-call(f32[8,64,128]{2,1,0:T(8,128)} %p_now.1, f32[8,64,128]{2,1,0:T(8,128)} %p_prev.1, f32[8,64,128]{2,1,0:T(8,128)} %velocity.1, f32[8,64,128]{2,1,0:T(8,128)} %density.1, ...), custom_call_target="tpu_custom_call" | custom-call | tf_op jit(solution)/shard_map/pallas_call | solution.py:696
  82.3 1.0 %shard_map.129 = (f32[8,64,128]{2,1,0:T(8,128)}, f32[16,256]{1,0:T(8,128)}, f32[1,128]{1,0:T(1,128)}, f32[8,8,128]{2,1,0:T(8,128)}, f32[3,8,64,128]{3,2,1,0:T(8,128)}) custom-call(f32[8,64,128]{2,1,0:T(8,128)S(1)} %get-tuple-element.15.refs_0_, f32[16,256]{1,0:T(8,128)S(1)} %get-tuple-element.16.refs_1_, f32[1,128]{1,0:T(1,128)S(1)} %get-tuple-element.17.refs_2_, ...), custom_call_target="tpu_custom_call" | custom-call | tf_op jit(solution)/shard_map/pallas_call | solution.py:742
Async XLA Ops:
  1.3 0.7 copy-start
